TPU v7x, 32 devices: a whole 2x2x4 slice. The times are simulated.
32 devices in a mesh: seq: 4 (over y, core), blk: 8 (over z, x).
Axes of the slice: x: 2, y: 2, z: 4, core: 2. Of those that a mesh axis runs over, the one named last changes fastest.
Arguments:
- hidden_states: bfloat16 [512, 4096], P('seq'), may hold values from -6 to 6
- query_weight: bfloat16 [4096, 4096], P('seq', 'blk')
- key_weight: bfloat16 [4096, 4096], P('seq', 'blk')
- value_weight: bfloat16 [4096, 4096], P('seq', 'blk'), may hold values from -0.09375 to 0.09375
- output_weight: bfloat16 [4096, 4096], P('blk', 'seq'), may hold values from -0.125 to 0.125
- query_gain: float32 [4096], P('blk'), may hold values from 0.7 to 3
- key_gain: float32 [4096], P('blk'), may hold values from 0.7 to 3
- attention_gain: float32 [4096], replicated, may hold values from 0.5 to 1.5
- gate_weight: bfloat16 [4096, 11008], P('seq', 'blk'), may hold values from -0.09375 to 0.09375
- up_weight: bfloat16 [4096, 11008], P('seq', 'blk'), may hold values from -0.09375 to 0.09375
- down_weight: bfloat16 [11008, 4096], P('blk', 'seq'), may hold values from -0.078125 to 0.078125
- feedforward_gain: float32 [4096], replicated, may hold values from 0.5 to 1.5
- cached_keys: bfloat16 [4, 1024, 4096], P('seq', None, 'blk'), may hold values from -6 to 6
- cached_values: bfloat16 [4, 1024, 4096], P('seq', None, 'blk'), may hold values from -6 to 6
- passage_order: int32 [4], replicated, may hold values from 0 to 3, each once
- separators: int32 [2, 2], replicated, may hold values from 1 to 64
- recompute_index: int32 [4, 96], replicated, may hold values from 0 to 1023, as said below
- prompt_lengths: int32 [2], replicated, may hold values from 16 to 64, as said below
Outputs:
- hidden_out: bfloat16 [512, 4096], P(('seq', 'blk'))
- blended_keys: bfloat16 [4, 1024, 4096], P('seq', None, 'blk')
- blended_values: bfloat16 [4, 1024, 4096], P('seq', None, 'blk')
Inputs may be any that keep to these rules, and one draw needn't show every extreme that they name: `passage_order`: each passage id appears once. `recompute_index`: distinct within each passage. `prompt_lengths`: some request has all 64 of its new tokens live.
All inputs are finite; a program needn't handle non-finite values.
Results may differ from a plain program's by a relative error of at most 0.035.
Values may be sent and summed in bfloat16 or wider, within the bound.
A program may use at most 128 MiB of HBM per device.

v0:
```python
import math

import jax
import jax.numpy as jnp
from jax import lax
from jax.sharding import PartitionSpec as P

HD = 128
PLEN = 1024
SEL = 96
PPR = 2
TOKN_DEV = 32


EPSILON = 1e-06
ROPE_THETA = 500000.0
MASKED_SCORE = -1e30


def joined(part, axis, combine):
    gathered = jax.tree.map(lambda a: lax.all_gather(a, axis), part)

    def take(source):
        return jax.tree.map(lambda a: lax.dynamic_index_in_dim(a, source, 0, False), gathered)

    return lax.fori_loop(
        1, lax.axis_size(axis), lambda source, state: combine(state, take(source)), take(0)
    )


def frequencies():
    indices = jnp.arange(HD // 2, dtype=jnp.float32)
    return jnp.exp(indices * (-2.0 * math.log(ROPE_THETA) / HD))


def rotate(values, angles):
    half_width = values.shape[-1] // 2
    cosine = jnp.cos(angles)[:, None, :]
    sine = jnp.sin(angles)[:, None, :]
    first = values[..., :half_width]
    second = values[..., half_width:]
    return jnp.concatenate(
        [first * cosine - second * sine, second * cosine + first * sine], axis=-1
    )


def normalize(matrix):
    return matrix * lax.rsqrt(jnp.mean(matrix * matrix, axis=-1, keepdims=True) + EPSILON)


def layout(passage_order, separators, recompute_index, prompt_lengths, seq_count):
    request_count = seq_count // PPR
    ordering = passage_order.reshape(request_count, PPR)
    slot_ids = jnp.arange(PPR, dtype=jnp.int32)
    opening = slot_ids[None, :] * PLEN + jnp.cumsum(separators, axis=1)
    flattened = ordering.reshape(-1)
    starts = jnp.zeros((seq_count,), jnp.int32).at[flattened].set(opening.reshape(-1))
    request_ids = jnp.repeat(jnp.arange(request_count, dtype=jnp.int32), PPR)
    owners = jnp.zeros((seq_count,), jnp.int32).at[flattened].set(request_ids)
    prompt_start = opening[:, PPR - 1] + PLEN
    devices = jnp.arange(seq_count, dtype=jnp.int32)
    new_request = devices // PPR
    new_index = (devices % PPR)[:, None] * TOKN_DEV + jnp.arange(TOKN_DEV, dtype=jnp.int32)[None, :]
    new_positions = prompt_start[new_request][:, None] + new_index
    new_live = new_index < prompt_lengths[new_request][:, None]
    picked_positions = starts[:, None] + recompute_index
    row_positions = jnp.concatenate([picked_positions, new_positions], axis=1).reshape(-1)
    row_live = jnp.concatenate([jnp.ones(picked_positions.shape, bool), new_live], axis=1).reshape(
        -1
    )
    return (starts, owners, row_positions, row_live)


def partial_attention(queries, key_block, value_block, visible, head_count):
    query_count = queries.shape[0]
    key_count = key_block.shape[0]
    query_heads = queries.reshape(query_count, head_count, HD)
    key_heads = key_block.reshape(key_count, head_count, HD)
    value_heads = value_block.reshape(key_count, head_count, HD)
    scores = jnp.einsum(
        "qhd,khd->hqk", query_heads, key_heads, preferred_element_type=jnp.float32
    ) * HD ** (-0.5)
    masked = jnp.where(visible[None], scores, MASKED_SCORE)
    peaks = jnp.max(masked, axis=2)
    exponentials = jnp.where(visible[None], jnp.exp(masked - peaks[:, :, None]), 0.0)
    totals = jnp.sum(exponentials, axis=2)
    weighted = jnp.einsum(
        "hqk,khd->qhd",
        exponentials.astype(jnp.bfloat16),
        value_heads,
        preferred_element_type=jnp.float32,
    )
    return (weighted, peaks.T, totals.T)


def spread(parts, indices, total_rows):
    weighted, peaks, totals = parts
    head_count = peaks.shape[1]
    full_weighted = jnp.zeros((total_rows, head_count, HD), jnp.float32).at[indices].set(weighted)
    full_peaks = (
        jnp.full((total_rows, head_count), MASKED_SCORE, jnp.float32).at[indices].set(peaks)
    )
    full_totals = jnp.zeros((total_rows, head_count), jnp.float32).at[indices].set(totals)
    return (full_weighted, full_peaks, full_totals)


def combine(first, second):
    peaks = jnp.maximum(first[1], second[1])
    first_factor = jnp.exp(first[1] - peaks)
    second_factor = jnp.exp(second[1] - peaks)
    weighted = first[0] * first_factor[:, :, None] + second[0] * second_factor[:, :, None]
    return (weighted, peaks, first[2] * first_factor + second[2] * second_factor)


def shards(
    hidden_states,
    query_weight,
    key_weight,
    value_weight,
    output_weight,
    query_gain,
    key_gain,
    attention_gain,
    gate_weight,
    up_weight,
    down_weight,
    feedforward_gain,
    cached_keys,
    cached_values,
    passage_order,
    separators,
    recompute_index,
    prompt_lengths,
):
    seq_count = lax.axis_size("seq")
    blk_count = lax.axis_size("blk")
    seq_index = lax.axis_index("seq")
    blk_index = lax.axis_index("blk")
    row_count = hidden_states.shape[0]
    local_width = query_weight.shape[1]
    head_count = local_width // HD
    total_rows = row_count * seq_count
    part_rows = row_count // blk_count
    starts, owners, row_positions, row_live = layout(
        passage_order, separators, recompute_index, prompt_lengths, seq_count
    )
    frequency = frequencies()
    pieces = (
        lax.all_gather(query_weight, "seq", axis=0, tiled=True),
        lax.all_gather(key_weight, "seq", axis=0, tiled=True),
        lax.all_gather(value_weight, "seq", axis=0, tiled=True),
    )
    query_raw = jnp.dot(hidden_states, pieces[0], preferred_element_type=jnp.float32)
    key_raw = jnp.dot(hidden_states, pieces[1], preferred_element_type=jnp.float32)
    value_raw = jnp.dot(hidden_states, pieces[2], preferred_element_type=jnp.float32)
    query_squares, key_squares = lax.psum(
        (jnp.sum(query_raw * query_raw, axis=1), jnp.sum(key_raw * key_raw, axis=1)), "blk"
    )
    full_width = local_width * blk_count
    my_positions = lax.dynamic_slice_in_dim(row_positions, seq_index * row_count, row_count)
    my_live = lax.dynamic_slice_in_dim(row_live, seq_index * row_count, row_count)
    angles = my_positions.astype(jnp.float32)[:, None] * frequency[None, :]
    query_scaled = query_raw * lax.rsqrt(query_squares / full_width + EPSILON)[:, None] * query_gain
    key_scaled = key_raw * lax.rsqrt(key_squares / full_width + EPSILON)[:, None] * key_gain
    query = (
        rotate(query_scaled.reshape(row_count, head_count, HD), angles)
        .reshape(row_count, local_width)
        .astype(jnp.bfloat16)
    )
    key_rows = (
        rotate(key_scaled.reshape(row_count, head_count, HD), angles)
        .reshape(row_count, local_width)
        .astype(jnp.bfloat16)
    )
    value_rows = value_raw.astype(jnp.bfloat16)
    passage_start = lax.dynamic_index_in_dim(starts, seq_index, 0, keepdims=False)
    turned = jnp.broadcast_to(passage_start.astype(jnp.float32) * frequency, (PLEN, HD // 2))
    old_keys = cached_keys[0].astype(jnp.float32).reshape(PLEN, head_count, HD)
    picked = lax.dynamic_index_in_dim(recompute_index, seq_index, 0, keepdims=False)
    passage_keys = (
        rotate(old_keys, turned)
        .reshape(PLEN, local_width)
        .astype(jnp.bfloat16)
        .at[picked]
        .set(key_rows[:SEL])
    )
    passage_values = cached_values[0].at[picked].set(value_rows[:SEL])
    all_queries = lax.all_gather(query, "seq", axis=0, tiled=True)
    request = lax.dynamic_index_in_dim(owners, seq_index, 0, keepdims=False)
    ordering = passage_order.reshape(-1, PPR)
    retrieved = lax.dynamic_index_in_dim(ordering, request, 0, keepdims=False)
    slot_ids = jnp.arange(PPR, dtype=jnp.int32)
    new_offsets = SEL + jnp.arange(TOKN_DEV, dtype=jnp.int32)
    picked_offsets = jnp.arange(SEL, dtype=jnp.int32)
    chosen_rows = (retrieved[:, None] * row_count + picked_offsets[None, :]).reshape(-1)
    group_rows = ((request * PPR + slot_ids)[:, None] * row_count + new_offsets[None, :]).reshape(
        -1
    )
    rows_first = jnp.concatenate([chosen_rows, group_rows])
    passage_positions = passage_start + jnp.arange(PLEN, dtype=jnp.int32)
    first_visible = passage_positions[None, :] <= row_positions[rows_first][:, None]
    first_parts = partial_attention(
        all_queries[rows_first], passage_keys, passage_values, first_visible, head_count
    )
    own_request = seq_index // PPR
    rows_second = (
        (own_request * PPR + slot_ids)[:, None] * row_count + new_offsets[None, :]
    ).reshape(-1)
    second_visible = (my_positions[SEL:][None, :] <= row_positions[rows_second][:, None]) & my_live[
        SEL:
    ][None, :]
    second_parts = partial_attention(
        all_queries[rows_second], key_rows[SEL:], value_rows[SEL:], second_visible, head_count
    )
    local_parts = combine(
        spread(first_parts, rows_first, total_rows), spread(second_parts, rows_second, total_rows)
    )
    merged = joined(local_parts, "seq", combine)
    weighted = lax.dynamic_slice_in_dim(merged[0], seq_index * row_count, row_count, 0)
    totals = lax.dynamic_slice_in_dim(merged[2], seq_index * row_count, row_count, 0)
    attention = (weighted / totals[:, :, None]).reshape(row_count, local_width).astype(jnp.bfloat16)
    gate_full, up_full, down_full = (
        lax.all_gather(gate_weight, "seq", axis=0, tiled=True),
        lax.all_gather(up_weight, "seq", axis=0, tiled=True),
        lax.all_gather(down_weight, "seq", axis=1, tiled=True),
    )
    output_full = lax.all_gather(output_weight, "seq", axis=1, tiled=True)
    summed = lax.psum_scatter(
        jnp.dot(attention, output_full, preferred_element_type=jnp.float32).astype(jnp.bfloat16),
        "blk",
        scatter_dimension=0,
        tiled=True,
    ).astype(jnp.float32)
    input_rows = lax.dynamic_slice_in_dim(hidden_states, blk_index * part_rows, part_rows, 0)
    mixed_rows = (input_rows.astype(jnp.float32) + normalize(summed) * attention_gain).astype(
        jnp.bfloat16
    )
    pieces = lax.all_gather(mixed_rows, "blk", axis=0, tiled=True)
    gate_values = jnp.dot(pieces, gate_full, preferred_element_type=jnp.float32)
    up_values = jnp.dot(pieces, up_full, preferred_element_type=jnp.float32)
    activation = (jax.nn.silu(gate_values) * up_values).astype(jnp.bfloat16)
    feedforward = lax.psum_scatter(
        jnp.dot(activation, down_full, preferred_element_type=jnp.float32).astype(jnp.bfloat16),
        "blk",
        scatter_dimension=0,
        tiled=True,
    ).astype(jnp.float32)
    hidden_out = (
        mixed_rows.astype(jnp.float32) + normalize(feedforward) * feedforward_gain
    ).astype(jnp.bfloat16)
    return (hidden_out, passage_keys[None], passage_values[None])


def solution(mesh):
    return jax.shard_map(
        shards,
        mesh=mesh,
        in_specs=(
            P("seq", None),
            P("seq", "blk"),
            P("seq", "blk"),
            P("seq", "blk"),
            P("blk", "seq"),
            P("blk"),
            P("blk"),
            P(),
            P("seq", "blk"),
            P("seq", "blk"),
            P("blk", "seq"),
            P(),
            P("seq", None, "blk"),
            P("seq", None, "blk"),
            P(),
            P(),
            P(),
            P(),
        ),
        out_specs=(P(("seq", "blk"), None), P("seq", None, "blk"), P("seq", None, "blk")),
        check_vma=False,
    )
```

profile of v0, /device:TPU:0, one launch (start us, length us, event | category | flops | bytes accessed | tf_op | source)
XLA Modules:
  0.0 661.2 jit_solution(17899709190707993705)
XLA Ops:
  24.8 22.0 %all-gather.15.cloned.1.call-done = bf16[4096,512]{1,0:T(8,128)(2,1)} async-done(((bf16[1024,512]{1,0:T(8,128)(2,1)}), bf16[4096,512]{1,0:T(8,128)(2,1)}) %all-gather.15.cloned.1.call-update) | async-done | bytes 4194320 | tf_op jit(solution)/shard_map/all_gather | solution.py:149
  49.9 33.0 %all-gather.17.cloned.1.call-done = bf16[4096,512]{1,0:T(8,128)(2,1)} async-done(((bf16[1024,512]{1,0:T(8,128)(2,1)}), bf16[4096,512]{1,0:T(8,128)(2,1)}) %all-gather.17.cloned.1.call-update) | async-done | bytes 4194320 | tf_op jit(solution)/shard_map/all_gather | solution.py:150
  85.9 21.4 %all-reduce.1 = (f32[128]{0:T(128)S(1)}, f32[128]{0:T(128)S(1)}) all-reduce(f32[128]{0:T(128)S(1)} %get-tuple-element.224, f32[128]{0:T(128)S(1)} %get-tuple-element.226), channel_id=1, replica_groups=mesh['seq'=4,'blk'=8] {'blk'}, use_global_device_ids=true, to_apply=%region_5.6 | all-reduce | flops 256 | bytes 2048 | tf_op jit(solution)/shard_map/psum | solution.py:156
  108.6 10.1 %all_gather.47 = bf16[512,512]{1,0:T(8,128)(2,1)S(1)} all-gather(bf16[128,512]{1,0:T(8,128)(2,1)S(1)} %copy.71), channel_id=1, replica_groups=mesh['seq'=4,'blk'=8] {'seq'}, dimensions={0}, use_global_device_ids=true | all-gather | bytes 655360 | tf_op jit(solution)/shard_map/all_gather | solution.py:188
  120.7 3.3 scatter_custom_fusion.3
  140.2 3.9 fusion.10
  147.8 7.0 %scatter_fusion = f32[512,4,128]{2,1,0:T(4,128)S(1)} fusion(f32[512,4,128]{2,1,0:T(4,128)S(1)} %broadcast.375.clone.1, s32[256]{0:T(256)S(1)} %bitcast.131, f32[256,4,128]{2,1,0:T(4,128)S(1)} %copy.80), kind=kCustom, calls=%fused_computation.10 | custom fusion | bytes 1573888 | tf_op jit(solution)/shard_map/scatter | solution.py:99
  162.5 13.7 %all-gather.1 = f32[2048,4]{1,0:T(8,128)S(1)} all-gather(f32[512,4]{1,0:T(8,128)} %get-tuple-element.205), channel_id=3, replica_groups=mesh['seq'=4,'blk'=8] {'seq'}, dimensions={0}, use_global_device_ids=true | all-gather | bytes 40960 | tf_op jit(solution)/shard_map/all_gather | solution.py:21
  176.2 16.1 %all-gather.2 = f32[2048,4]{1,0:T(8,128)S(1)} all-gather(f32[512,4]{1,0:T(8,128)S(1)} %get-tuple-element.202), channel_id=4, replica_groups=mesh['seq'=4,'blk'=8] {'seq'}, dimensions={0}, use_global_device_ids=true | all-gather | bytes 40960 | tf_op jit(solution)/shard_map/all_gather | solution.py:21
  193.4 8.3 %all-gather.29.cloned.1.call-done = f32[2048,4,128]{2,1,0:T(4,128)} async-done(((f32[512,4,128]{2,1,0:T(4,128)}), f32[2048,4,128]{2,1,0:T(4,128)}) %all-gather.29.cloned.1.call-update) | async-done | bytes 4194320 | tf_op jit(solution)/shard_map/all_gather | solution.py:21
  203.0 14.9 %while.19 = (s32[]{:T(128)}, f32[512,4,128]{2,1,0:T(4,128)S(1)}, f32[512,4]{1,0:T(8,128)S(1)}, f32[512,4]{1,0:T(8,128)S(1)}, f32[4,512,4]{2,1,0:T(8,128)}, /*ind...) while((s32[]{:T(128)}, f32[512,4,128]{2,1,0:T(4,128)S(1)}, ...), condition=%wide.region_20.21_spmd, body=%wide.region_19.20_spmd.sunk | while | flops 798725 | bytes 3227799 | solution.py:26
  204.3 3.7 fusion.101
  209.3 3.7 fusion.101
  214.2 3.6 fusion.101
  218.1 16.6 %all-gather.19.cloned.1.call-done = bf16[512,4096]{1,0:T(8,128)(2,1)} async-done(((bf16[512,1024]{1,0:T(8,128)(2,1)}), bf16[512,4096]{1,0:T(8,128)(2,1)}) %all-gather.19.cloned.1.call-update) | async-done | bytes 4194320 | tf_op jit(solution)/shard_map/all_gather | solution.py:227
  234.7 3.9 convolution_convert_fusion.1
  238.7 63.6 %reduce-scatter.3.cloned.1.call-done = bf16[16,4096]{1,0:T(8,128)(2,1)} async-done(((bf16[128,4096]{1,0:T(8,128)(2,1)}), bf16[16,4096]{1,0:T(8,128)(2,1)}) %reduce-scatter.3.cloned.1.call-update) | async-done | bytes 131088 | tf_op jit(solution)/shard_map/reduce_scatter | solution.py:228
  307.4 37.1 %all-gather.21.cloned.1.call-done = bf16[128,4096]{1,0:T(8,128)(2,1)} async-done(((bf16[16,4096]{1,0:T(8,128)(2,1)}), bf16[128,4096]{1,0:T(8,128)(2,1)}) %all-gather.21.cloned.1.call-update) | async-done | bytes 1048592 | tf_op jit(solution)/shard_map/all_gather | solution.py:238
  344.4 75.1 %all-gather.23.cloned.1.call-done = bf16[4096,1376]{0,1:T(8,128)(2,1)} async-done(((bf16[1024,1376]{0,1:T(8,128)(2,1)}), bf16[4096,1376]{0,1:T(8,128)(2,1)}) %all-gather.23.cloned.1.call-update) | async-done | bytes 11272208 | tf_op jit(solution)/shard_map/all_gather | solution.py:223
  419.5 6.2 fusion.81
  425.8 70.1 %all-gather.25.cloned.1.call-done = bf16[4096,1376]{0,1:T(8,128)(2,1)} async-done(((bf16[1024,1376]{0,1:T(8,128)(2,1)}), bf16[4096,1376]{0,1:T(8,128)(2,1)}) %all-gather.25.cloned.1.call-update) | async-done | bytes 11272208 | tf_op jit(solution)/shard_map/all_gather | solution.py:224
  495.9 76.2 %all-gather.27.cloned.1.call-done = bf16[1376,4096]{1,0:T(8,128)(2,1)} async-done(((bf16[1376,1024]{1,0:T(8,128)(2,1)}), bf16[1376,4096]{1,0:T(8,128)(2,1)}) %all-gather.27.cloned.1.call-update) | async-done | bytes 11272208 | tf_op jit(solution)/shard_map/all_gather | solution.py:225
  572.1 16.3 %convolution_convert_fusion = bf16[128,4096]{1,0:T(8,128)(2,1)} fusion(bf16[1376,4096]{1,0:T(8,128)(2,1)} %all-gather.27.cloned.1.call-done, bf16[128,4096]{1,0:T(8,128)(2,1)S(1)} %copy-done.5, bf16[4096,1376]{0,1:T(8,128)(2,1)} %all-gather.25.cloned.1.call-done, f32[128,1376]{0,1:T(8,128)S(1)} %fusion.81), kind=kOutput, calls=%fused_computation.24 | convolution fusion | flops 2887262208 | bytes 25346048 | tf_op jit(solution)/shard_map/dot_general | solution.py:243
  588.4 63.5 %reduce-scatter.5.cloned.1.call-done = bf16[16,4096]{1,0:T(8,128)(2,1)} async-done(((bf16[128,4096]{1,0:T(8,128)(2,1)}), bf16[16,4096]{1,0:T(8,128)(2,1)}) %reduce-scatter.5.cloned.1.call-update) | async-done | bytes 131088 | tf_op jit(solution)/shard_map/reduce_scatter | solution.py:242
  (165 shorter events, 65.2 us)
Async XLA Ops:
  7.2 15.4 %copy-start = (s32[2]{0:T(128)S(1)}, s32[2]{0:T(128)}, u32[]{:S(2)}) copy-start(s32[2]{0:T(128)} %param.37) | copy-start | bytes 28
  7.2 8.1 %copy-start.10 = (bf16[1,1024,512]{2,1,0:T(8,128)(2,1)S(1)}, bf16[1,1024,512]{2,1,0:T(8,128)(2,1)}, u32[]{:S(2)}) copy-start(bf16[1,1024,512]{2,1,0:T(8,128)(2,1)} %param.32) | copy-start | bytes 3145732
  7.2 39.6 %all-gather.15.cloned.1.call-start = ((), (), s32[]{:S(2)}) async-start(), calls=%async_computation.3 | async-start | bytes 5242880 | tf_op jit(solution)/shard_map/all_gather | solution.py:149
  7.9 75.0 %all-gather.17.cloned.1.call-start = ((), (), s32[]{:S(2)}) async-start(), calls=%async_computation.4 | async-start | bytes 5242880 | tf_op jit(solution)/shard_map/all_gather | solution.py:150
  8.7 125.1 %all-gather.13.cloned.1.call-start = ((), (), s32[]{:S(2)}) async-start(), calls=%async_computation.2 | async-start | bytes 5242880 | tf_op jit(solution)/shard_map/all_gather | solution.py:151
  9.4 192.3 %all-gather.29.cloned.1.call-start = ((), (), s32[]{:S(2)}) async-start(), calls=%async_computation.12 | async-start | bytes 5242880 | tf_op jit(solution)/shard_map/all_gather | solution.py:21
  17.2 29.6 %copy-start.2 = (bf16[128,4096]{1,0:T(8,128)(2,1)S(1)}, bf16[128,4096]{1,0:T(8,128)(2,1)}, u32[]{:S(2)}) copy-start(bf16[128,4096]{1,0:T(8,128)(2,1)} %param.20) | copy-start | bytes 3145732
  24.8 82.5 %copy-start.13 = (f32[512]{0:T(512)S(1)}, f32[512]{0:T(512)}, u32[]{:S(2)}) copy-start(f32[512]{0:T(512)} %param.26) | copy-start | bytes 6148
  49.9 57.6 %copy-start.14 = (f32[512]{0:T(512)S(1)}, f32[512]{0:T(512)}, u32[]{:S(2)}) copy-start(f32[512]{0:T(512)} %param.25) | copy-start | bytes 6148
  129.8 7.2 %copy-start.8 = (bf16[1,1024,512]{2,1,0:T(8,128)(2,1)S(1)}, bf16[1,1024,512]{2,1,0:T(8,128)(2,1)}, u32[]{:S(2)}) copy-start(bf16[1,1024,512]{2,1,0:T(8,128)(2,1)} %param.33) | copy-start | bytes 3145732
  138.8 5.3 copy-start.7
  161.9 72.8 %all-gather.19.cloned.1.call-start = ((), (), s32[]{:S(2)}) async-start(), calls=%async_computation.5 | async-start | bytes 5242880 | tf_op jit(solution)/shard_map/all_gather | solution.py:227
  162.5 139.8 %reduce-scatter.3.cloned.1.call-start = ((), (), s32[]{:S(2)}) async-start(), calls=%async_computation.6 | async-start | bytes 1179648 | tf_op jit(solution)/shard_map/reduce_scatter | solution.py:228
  176.2 17.2 %copy-start.3 = (f32[2048,4]{1,0:T(8,128)}, f32[2048,4]{1,0:T(8,128)S(1)}, u32[]{:S(2)}) copy-start(f32[2048,4]{1,0:T(8,128)S(1)} %all-gather.1) | copy-start | bytes 98308
  217.9 85.5 %copy-start.11 = (f32[4096]{0:T(1024)S(1)}, f32[4096]{0:T(1024)}, u32[]{:S(2)}) copy-start(f32[4096]{0:T(1024)} %param.27) | copy-start | bytes 49156
  238.6 105.8 %all-gather.21.cloned.1.call-start = ((), (), s32[]{:S(2)}) async-start(), calls=%async_computation.7 | async-start | bytes 1179648 | tf_op jit(solution)/shard_map/all_gather | solution.py:238
  305.0 114.5 %all-gather.23.cloned.1.call-start = ((), (), s32[]{:S(2)}) async-start(), calls=%async_computation.8 | async-start | bytes 14090240 | tf_op jit(solution)/shard_map/all_gather | solution.py:223
  305.8 190.1 %all-gather.25.cloned.1.call-start = ((), (), s32[]{:S(2)}) async-start(), calls=%async_computation.9 | async-start | bytes 14090240 | tf_op jit(solution)/shard_map/all_gather | solution.py:224
  306.5 265.5 %all-gather.27.cloned.1.call-start = ((), (), s32[]{:S(2)}) async-start(), calls=%async_computation.10 | async-start | bytes 14090240 | tf_op jit(solution)/shard_map/all_gather | solution.py:225
  307.1 344.8 %reduce-scatter.5.cloned.1.call-start = ((), (), s32[]{:S(2)}) async-start(), calls=%async_computation.11 | async-start | bytes 1179648 | tf_op jit(solution)/shard_map/reduce_scatter | solution.py:242
  344.4 227.6 %copy-start.5 = (bf16[128,4096]{1,0:T(8,128)(2,1)S(1)}, bf16[128,4096]{1,0:T(8,128)(2,1)}, u32[]{:S(2)}) copy-start(bf16[128,4096]{1,0:T(8,128)(2,1)} %all-gather.21.cloned.1.call-done) | copy-start | bytes 3145732
  425.7 227.2 %copy-start.9 = (bf16[16,4096]{1,0:T(8,128)(2,1)S(1)}, bf16[16,4096]{1,0:T(8,128)(2,1)}, u32[]{:S(2)}) copy-start(bf16[16,4096]{1,0:T(8,128)(2,1)} %fusion.21) | copy-start | bytes 393220
  425.7 227.2 %copy-start.12 = (f32[4096]{0:T(1024)S(1)}, f32[4096]{0:T(1024)}, u32[]{:S(2)}) copy-start(f32[4096]{0:T(1024)} %param.31) | copy-start | bytes 49156
  572.1 82.6 %copy-start.1 = (s32[2]{0:T(128)S(1)}, s32[2]{0:T(128)}, u32[]{:S(2)}) copy-start(s32[2]{0:T(128)} %param.37) | copy-start | bytes 28
  (5 other events, 11.8 us)
Sparse Core Ops, SparseCore 0:
  9.6 37.1 all-gather.14
  48.4 34.4 all-gather.16
  84.5 37.2 all-gather.12
  162.0 39.6 all-gather.28
  203.1 31.5 all-gather.18
  238.7 63.4 reduce-scatter.2
  305.2 39.2 all-gather.20
  346.1 73.4 all-gather.22
  421.2 74.6 all-gather.24
  497.4 74.6 all-gather.26
  588.5 63.3 reduce-scatter.4
where the time goes:
time: 662 us; the launch traced here: 661 us
  waiting for transfers between devices  470 us (71%)
  blocking collectives  61.3 us (9%)
  matrix products  42 us (6%)
  local copies, waits for them, and re-layouts  39.4 us (6%)
  other arithmetic  30 us (5%)
  between operations  17.7 us (3%)
    all_gather x1, waiting for transfers between devices, shards(): lax.all_gather(down_weight, 'seq', axis=1, tiled=True)  76.2 us
    all_gather x1, waiting for transfers between devices, shards(): lax.all_gather(gate_weight, 'seq', axis=0, tiled=True)  75.1 us
    all_gather x1, waiting for transfers between devices, shards(): lax.all_gather(up_weight, 'seq', axis=0, tiled=True)  70.1 us
    reduce_scatter x1, waiting for transfers between devices, shards(): lax.psum_scatter(jnp.dot(attention, output_full, preferred_element_type=j...  63.6 us
    reduce_scatter x1, waiting for transfers between devices, shards(): lax.psum_scatter(jnp.dot(activation, down_full, preferred_element_type=jn...  63.5 us
    all_gather x1, waiting for transfers between devices, shards(): pieces = lax.all_gather(mixed_rows, 'blk', axis=0, tiled=True)  37.1 us
    all_gather x1, waiting for transfers between devices, shards(): lax.all_gather(key_weight, 'seq', axis=0, tiled=True)  33 us
    all_gather x2, blocking collectives, joined(): gathered = jax.tree.map(lambda a: lax.all_gather(a, axis), part)  29.8 us
  transfers between devices with their start and end apart: 11, of which 10 were waited for; matrix products, arithmetic and copies ran while one was open for 8% of the time, Pallas kernels for 0%

commit v1 on v0

v1 whole, which is shorter than its diff:
```python
import functools
import math

import jax
import jax.numpy as jnp
from jax import lax
from jax.experimental import pallas as pl
from jax.experimental.pallas import tpu as pltpu
from jax.sharding import PartitionSpec as P

HD = 128
PLEN = 1024
SEL = 96
PPR = 2
TOKN_DEV = 32

EPSILON = 1e-06
ROPE_THETA = 500000.0
MASKED_SCORE = -1e30
MESH = pl.DeviceIdType.MESH
ANY = pl.BlockSpec(memory_space=pl.ANY)
VMEM = pl.BlockSpec(memory_space=pltpu.VMEM)


def greet(peers):
    barrier = pltpu.get_barrier_semaphore()
    for peer in peers:
        pl.semaphore_signal(barrier, inc=1, device_id=peer, device_id_type=MESH)
    pl.semaphore_wait(barrier, len(peers))


def peers_of(axis, count):
    me = lax.axis_index(axis)
    return [{axis: lax.rem(me + offset, count)} for offset in range(1, count)]


def send(source, target, send_sem, recv_sem, peer):
    copy = pltpu.make_async_remote_copy(
        src_ref=source,
        dst_ref=target,
        send_sem=send_sem,
        recv_sem=recv_sem,
        device_id=peer,
        device_id_type=MESH,
    )
    copy.start()
    return copy


def exchange_kernel(axis, count, array_count, scatter, *refs):
    sources, targets = refs[:array_count], refs[array_count : 2 * array_count]
    send_sems, recv_sems, local_sems = refs[2 * array_count :]
    me = lax.axis_index(axis)
    peers = peers_of(axis, count)
    greet(peers)
    copies = []
    for offset in range(1, count):
        for k in range(array_count):
            peer = peers[offset - 1]
            source = sources[k].at[peer[axis]] if scatter else sources[k]
            copies.append(
                send(
                    source,
                    targets[k].at[me],
                    send_sems.at[k, offset],
                    recv_sems.at[k, offset],
                    peer,
                )
            )
    for k in range(array_count):
        source = sources[k].at[me] if scatter else sources[k]
        copy = pltpu.make_async_copy(source, targets[k].at[me], local_sems.at[k])
        copy.start()
        copies.append(copy)
    for copy in copies:
        copy.wait()


def exchange(axis, arrays, scatter, collective_id):
    count = lax.axis_size(axis)
    shapes = [
        jax.ShapeDtypeStruct(a.shape if scatter else (count,) + a.shape, a.dtype) for a in arrays
    ]
    return pl.pallas_call(
        functools.partial(exchange_kernel, axis, count, len(arrays), scatter),
        out_shape=shapes,
        in_specs=[ANY] * len(arrays),
        out_specs=[ANY] * len(arrays),
        scratch_shapes=[
            pltpu.SemaphoreType.DMA((len(arrays), count)),
            pltpu.SemaphoreType.DMA((len(arrays), count)),
            pltpu.SemaphoreType.DMA((len(arrays),)),
        ],
        compiler_params=pltpu.CompilerParams(collective_id=collective_id, has_side_effects=True),
    )(*arrays)


def gather_kernel(
    axis,
    count,
    sum_axis,
    sum_count,
    data_ref,
    squares_ref,
    gathered_ref,
    sums_ref,
    landing,
    data_send,
    data_recv,
    part_send,
    part_recv,
    sum_send,
    sum_recv,
    local_sem,
):
    me = lax.axis_index(axis)
    peers = peers_of(axis, count)
    sum_peers = peers_of(sum_axis, sum_count)
    greet(peers + sum_peers)
    parts = [
        send(
            squares_ref,
            landing.at[offset],
            part_send.at[offset],
            part_recv.at[offset],
            sum_peers[offset - 1],
        )
        for offset in range(1, sum_count)
    ]
    copies = [
        send(
            data_ref,
            gathered_ref.at[me],
            data_send.at[offset],
            data_recv.at[offset],
            peers[offset - 1],
        )
        for offset in range(1, count)
    ]
    local = pltpu.make_async_copy(data_ref, gathered_ref.at[me], local_sem)
    local.start()
    total = squares_ref[...]
    for offset in range(1, sum_count):
        parts[offset - 1].wait()
        total += landing[offset]
    sums_ref[me] = total
    for offset in range(1, count):
        copies.append(
            send(
                sums_ref.at[me],
                sums_ref.at[me],
                sum_send.at[offset],
                sum_recv.at[offset],
                peers[offset - 1],
            )
        )
    for copy in copies:
        copy.wait()
    local.wait()


def gather_with_sums(data, squares, axis, sum_axis, collective_id):
    count, sum_count = lax.axis_size(axis), lax.axis_size(sum_axis)
    return pl.pallas_call(
        functools.partial(gather_kernel, axis, count, sum_axis, sum_count),
        out_shape=[
            jax.ShapeDtypeStruct((count,) + data.shape, data.dtype),
            jax.ShapeDtypeStruct((count,) + squares.shape, squares.dtype),
        ],
        in_specs=[ANY, VMEM],
        out_specs=[ANY, VMEM],
        scratch_shapes=[
            pltpu.VMEM((sum_count,) + squares.shape, squares.dtype),
            pltpu.SemaphoreType.DMA((count,)),
            pltpu.SemaphoreType.DMA((count,)),
            pltpu.SemaphoreType.DMA((sum_count,)),
            pltpu.SemaphoreType.DMA((sum_count,)),
            pltpu.SemaphoreType.DMA((count,)),
            pltpu.SemaphoreType.DMA((count,)),
            pltpu.SemaphoreType.DMA,
        ],
        compiler_params=pltpu.CompilerParams(collective_id=collective_id, has_side_effects=True),
    )(data, squares)


def attention_kernel(
    query_ref,
    factor_ref,
    old_limit_ref,
    new_limit_ref,
    picked_ref,
    turn_ref,
    old_keys_ref,
    old_values_ref,
    key_rows_ref,
    value_rows_ref,
    keys_ref,
    values_ref,
    weighted_ref,
    stats_ref,
):
    @pl.when(pl.program_id(1) == 0)
    def blend():
        row_count = key_rows_ref.shape[0]
        token = lax.broadcasted_iota(jnp.int32, (PLEN, row_count), 0)
        hit = token == picked_ref[...]
        chosen = jnp.where(hit, 1.0, 0.0)
        replaced = jnp.max(chosen, axis=1, keepdims=True) > 0.5
        chosen = chosen.astype(jnp.bfloat16)
        old = old_keys_ref[...].astype(jnp.float32)
        turned = old * turn_ref[0:1, :] + pltpu.roll(old, HD // 2, 1) * turn_ref[1:2, :]
        new_keys = jnp.dot(chosen, key_rows_ref[...], preferred_element_type=jnp.float32)
        keys_ref[...] = jnp.where(replaced, new_keys, turned).astype(jnp.bfloat16)
        new_values = jnp.dot(chosen, value_rows_ref[...], preferred_element_type=jnp.float32)
        values_ref[...] = jnp.where(
            replaced, new_values, old_values_ref[...].astype(jnp.float32)
        ).astype(jnp.bfloat16)

    query = (query_ref[...].astype(jnp.float32) * factor_ref[...]).astype(jnp.bfloat16)
    contract = (((1,), (1,)), ((), ()))
    old_scores = lax.dot_general(
        query, keys_ref[...], contract, preferred_element_type=jnp.float32
    )
    new_scores = lax.dot_general(
        query, key_rows_ref[...], contract, preferred_element_type=jnp.float32
    )
    scale = HD ** (-0.5)
    old_seen = lax.broadcasted_iota(jnp.int32, old_scores.shape, 1) <= old_limit_ref[...]
    new_token = lax.broadcasted_iota(jnp.int32, new_scores.shape, 1) - SEL
    new_seen = (new_token >= 0) & (new_token <= new_limit_ref[...])
    old_scores = jnp.where(old_seen, old_scores * scale, MASKED_SCORE)
    new_scores = jnp.where(new_seen, new_scores * scale, MASKED_SCORE)
    peak = jnp.maximum(
        jnp.max(old_scores, axis=1, keepdims=True), jnp.max(new_scores, axis=1, keepdims=True)
    )
    old_weights = jnp.where(old_seen, jnp.exp(old_scores - peak), 0.0)
    new_weights = jnp.where(new_seen, jnp.exp(new_scores - peak), 0.0)
    total = jnp.sum(old_weights, axis=1, keepdims=True) + jnp.sum(
        new_weights, axis=1, keepdims=True
    )
    weighted = jnp.dot(
        old_weights.astype(jnp.bfloat16), values_ref[...], preferred_element_type=jnp.float32
    ) + jnp.dot(
        new_weights.astype(jnp.bfloat16), value_rows_ref[...], preferred_element_type=jnp.float32
    )
    weighted_ref[...] = weighted.astype(jnp.bfloat16)
    lane = lax.broadcasted_iota(jnp.int32, weighted.shape, 1)
    stats = jnp.transpose(jnp.where(lane == 0, peak, total))
    stats_ref[0] = stats[:8, :]


def attend(
    queries, factor, old_limit, new_limit, picked, turn, old_keys, old_values, key_rows, value_rows
):
    total_rows, width = queries.shape
    row_count = key_rows.shape[0]
    head_count = width // HD
    block = min(total_rows, 512)
    by_row = pl.BlockSpec((block, 1), lambda h, i: (i, 0))
    by_head = pl.BlockSpec((PLEN, HD), lambda h, i: (0, h))
    rows_by_head = pl.BlockSpec((row_count, HD), lambda h, i: (0, h))
    tile = pl.BlockSpec((block, HD), lambda h, i: (i, h))
    return pl.pallas_call(
        attention_kernel,
        grid=(head_count, total_rows // block),
        out_shape=[
            jax.ShapeDtypeStruct((PLEN, width), jnp.bfloat16),
            jax.ShapeDtypeStruct((PLEN, width), jnp.bfloat16),
            jax.ShapeDtypeStruct((total_rows, width), jnp.bfloat16),
            jax.ShapeDtypeStruct((head_count, 8, total_rows), jnp.float32),
        ],
        in_specs=[
            tile,
            by_row,
            by_row,
            by_row,
            pl.BlockSpec((1, row_count), lambda h, i: (0, 0)),
            pl.BlockSpec((8, HD), lambda h, i: (0, 0)),
            by_head,
            by_head,
            rows_by_head,
            rows_by_head,
        ],
        out_specs=[
            by_head,
            by_head,
            tile,
            pl.BlockSpec((1, 8, block), lambda h, i: (h, 0, i)),
        ],
        compiler_params=pltpu.CompilerParams(vmem_limit_bytes=48 * 1024 * 1024),
    )(
        queries,
        factor,
        old_limit,
        new_limit,
        picked,
        turn,
        old_keys,
        old_values,
        key_rows,
        value_rows,
    )


def frequencies():
    indices = jnp.arange(HD // 2, dtype=jnp.float32)
    return jnp.exp(indices * (-2.0 * math.log(ROPE_THETA) / HD))


def rotate(values, angles):
    half_width = values.shape[-1] // 2
    cosine = jnp.cos(angles)[:, None, :]
    sine = jnp.sin(angles)[:, None, :]
    first = values[..., :half_width]
    second = values[..., half_width:]
    return jnp.concatenate(
        [first * cosine - second * sine, second * cosine + first * sine], axis=-1
    )


def layout(passage_order, separators, recompute_index, seq_count):
    devices = jnp.arange(seq_count, dtype=jnp.int32)
    slots = jnp.arange(PPR, dtype=jnp.int32)
    earlier = slots[None, :, None] >= slots[None, None, :]
    opening = slots[None, :] * PLEN + jnp.sum(
        jnp.where(earlier, separators[:, None, :], 0), axis=2
    )
    hit = passage_order[None, :] == devices[:, None]
    starts = jnp.sum(jnp.where(hit, opening.reshape(-1)[None, :], 0), axis=1)
    owners = jnp.sum(jnp.where(hit, (devices // PPR)[None, :], 0), axis=1)
    prompt_start = jnp.repeat(opening[:, PPR - 1] + PLEN, PPR)
    offsets = (devices % PPR) * TOKN_DEV
    new_starts = prompt_start + offsets
    new_positions = new_starts[:, None] + jnp.arange(TOKN_DEV, dtype=jnp.int32)[None, :]
    positions = jnp.concatenate([starts[:, None] + recompute_index, new_positions], axis=1)
    requests = jnp.concatenate(
        [
            jnp.broadcast_to(owners[:, None], recompute_index.shape),
            jnp.broadcast_to((devices // PPR)[:, None], new_positions.shape),
        ],
        axis=1,
    )
    return starts, owners, new_starts, offsets, positions, requests


def total_of(parts):
    return jnp.sum(parts.astype(jnp.float32), axis=0)


def shards(
    hidden_states,
    query_weight,
    key_weight,
    value_weight,
    output_weight,
    query_gain,
    key_gain,
    attention_gain,
    gate_weight,
    up_weight,
    down_weight,
    feedforward_gain,
    cached_keys,
    cached_values,
    passage_order,
    separators,
    recompute_index,
    prompt_lengths,
):
    seq_count = lax.axis_size("seq")
    blk_count = lax.axis_size("blk")
    seq_index = lax.axis_index("seq")
    blk_index = lax.axis_index("blk")
    row_count, model_width = hidden_states.shape
    depth, local_width = query_weight.shape
    head_count = local_width // HD
    total_rows = row_count * seq_count
    part_rows = row_count // blk_count
    full_width = local_width * blk_count

    def mine(array):
        return lax.dynamic_index_in_dim(array, seq_index, 0, keepdims=False)

    starts, owners, new_starts, offsets, positions, requests = layout(
        passage_order, separators, recompute_index, seq_count
    )
    frequency = frequencies()
    passage_start = mine(starts)
    own_request = seq_index // PPR
    old_limit = jnp.where(requests == mine(owners), positions - passage_start, -1)
    live_limit = lax.dynamic_index_in_dim(prompt_lengths, own_request, 0, False) - 1 - mine(offsets)
    new_limit = jnp.where(
        requests == own_request, jnp.minimum(positions - mine(new_starts), live_limit), -1
    )
    picked = jnp.concatenate(
        [mine(recompute_index), jnp.full((row_count - SEL,), -1, jnp.int32)]
    ).reshape(1, row_count)
    turn_angles = passage_start.astype(jnp.float32) * frequency
    turn_cosine, turn_sine = jnp.cos(turn_angles), jnp.sin(turn_angles)
    turn = jnp.concatenate(
        [
            jnp.concatenate([turn_cosine, turn_cosine])[None],
            jnp.concatenate([-turn_sine, turn_sine])[None],
            jnp.zeros((6, HD), jnp.float32),
        ]
    )
    angles = mine(positions).astype(jnp.float32)[:, None] * frequency[None, :]

    columns = hidden_states.reshape(row_count, seq_count, depth).transpose(1, 0, 2)
    (hidden,) = exchange("seq", [columns], True, 0)
    hidden = hidden.reshape(total_rows, depth)

    def partial(rows, weight):
        product = jnp.dot(rows, weight, preferred_element_type=jnp.float32)
        return product.astype(jnp.bfloat16).reshape(seq_count, row_count, weight.shape[1])

    query_raw, key_raw, value_raw = (
        total_of(parts)
        for parts in exchange(
            "seq",
            [
                partial(hidden, query_weight),
                partial(hidden, key_weight),
                partial(hidden, value_weight),
            ],
            True,
            1,
        )
    )
    squares = jnp.concatenate(
        [
            jnp.sum(query_raw * query_raw, axis=1)[None],
            jnp.sum(key_raw * key_raw, axis=1)[None],
            jnp.zeros((6, row_count), jnp.float32),
        ]
    )

    def turned(raw, gain):
        return rotate((raw * gain).reshape(row_count, head_count, HD), angles).reshape(
            row_count, local_width
        )

    queries, sums = gather_with_sums(
        turned(query_raw, query_gain).astype(jnp.bfloat16), squares, "seq", "blk", 2
    )
    factors = lax.rsqrt(sums[:, :2] / full_width + EPSILON)
    key_rows = (turned(key_raw, key_gain) * mine(factors)[1][:, None]).astype(jnp.bfloat16)
    value_rows = value_raw.astype(jnp.bfloat16)
    passage_keys, passage_values, weighted, stats = attend(
        queries.reshape(total_rows, local_width),
        factors[:, 0].reshape(total_rows, 1),
        old_limit.reshape(total_rows, 1),
        new_limit.reshape(total_rows, 1),
        picked,
        turn,
        cached_keys[0],
        cached_values[0],
        key_rows,
        value_rows,
    )
    stats = (
        stats[:, :2]
        .reshape(head_count, 2, seq_count, row_count)
        .transpose(2, 1, 0, 3)
        .reshape(seq_count, 2 * head_count, row_count)
    )
    weighted, stats = exchange(
        "seq", [weighted.reshape(seq_count, row_count, local_width), stats], True, 3
    )
    peaks, totals = stats[:, :head_count], stats[:, head_count:]
    shares = jnp.exp(peaks - jnp.max(peaks, axis=0))
    shares = shares / jnp.sum(shares * totals, axis=0)
    shares = shares.transpose(0, 2, 1)[..., None]
    attention = (
        jnp.sum(
            weighted.astype(jnp.float32).reshape(seq_count, row_count, head_count, HD) * shares,
            axis=0,
        )
        .reshape(row_count, local_width)
        .astype(jnp.bfloat16)
    )
    (attention,) = exchange("seq", [attention], False, 4)

    def by_block(rows):
        return rows.reshape(seq_count, blk_count, part_rows, depth).transpose(1, 0, 2, 3)

    projected = jnp.dot(
        attention.reshape(total_rows, local_width),
        output_weight,
        preferred_element_type=jnp.float32,
    ).astype(jnp.bfloat16)
    (summed,) = exchange("blk", [by_block(projected)], True, 5)
    summed = total_of(summed)
    summed_squares = jnp.sum(summed * summed, axis=2).reshape(1, -1)
    summed_squares = jnp.pad(
        summed_squares, ((0, 7), (0, -summed_squares.shape[1] % 128))
    )
    summed, sums = gather_with_sums(
        summed.astype(jnp.bfloat16), summed_squares, "blk", "seq", 6
    )
    sums = sums[:, 0, : seq_count * part_rows].reshape(blk_count, seq_count, part_rows)
    factors = lax.rsqrt(sums / model_width + EPSILON)
    my_gain = lax.dynamic_slice_in_dim(attention_gain, seq_index * depth, depth)
    update = (summed.astype(jnp.float32) * factors[..., None] * my_gain).transpose(1, 0, 2, 3)
    mixed = (
        hidden.reshape(seq_count, blk_count, part_rows, depth).astype(jnp.float32) + update
    ).astype(jnp.bfloat16)
    mixed_rows = mixed.reshape(total_rows, depth)
    gate_values, up_values = (
        total_of(parts)
        for parts in exchange(
            "seq", [partial(mixed_rows, gate_weight), partial(mixed_rows, up_weight)], True, 7
        )
    )
    activation = (jax.nn.silu(gate_values) * up_values).astype(jnp.bfloat16)
    (activation,) = exchange("seq", [activation], False, 8)
    product = jnp.dot(
        activation.reshape(total_rows, -1), down_weight, preferred_element_type=jnp.float32
    ).astype(jnp.bfloat16)
    (feedforward,) = exchange("blk", [by_block(product)], True, 9)
    feedforward = total_of(feedforward).astype(jnp.bfloat16)
    my_mixed = lax.dynamic_index_in_dim(mixed, blk_index, 1, keepdims=False)
    feedforward, my_mixed = exchange("seq", [feedforward, my_mixed], True, 10)

    def whole(parts):
        return parts.astype(jnp.float32).transpose(1, 0, 2).reshape(part_rows, model_width)

    feedforward = whole(feedforward)
    normalized = feedforward * lax.rsqrt(
        jnp.mean(feedforward * feedforward, axis=-1, keepdims=True) + EPSILON
    )
    hidden_out = (whole(my_mixed) + normalized * feedforward_gain).astype(jnp.bfloat16)
    return (hidden_out, passage_keys[None], passage_values[None])


def solution(mesh):
    return jax.shard_map(
        shards,
        mesh=mesh,
        in_specs=(
            P("seq", None),
            P("seq", "blk"),
            P("seq", "blk"),
            P("seq", "blk"),
            P("blk", "seq"),
            P("blk"),
            P("blk"),
            P(),
            P("seq", "blk"),
            P("seq", "blk"),
            P("blk", "seq"),
            P(),
            P("seq", None, "blk"),
            P("seq", None, "blk"),
            P(),
            P(),
            P(),
            P(),
        ),
        out_specs=(P(("seq", "blk"), None), P("seq", None, "blk"), P("seq", None, "blk")),
        check_vma=False,
    )
```

time: 662 us -> 316 us (0.48)
  the two profiles are of different devices: /device:TPU:0 before, /device:TPU:15 now
where the time goes in v1:
time: 316 us; the launch traced here: 314 us
  Pallas kernels  217 us (69%)
  local copies, waits for them, and re-layouts  38 us (12%)
  other arithmetic  36.8 us (12%)
  matrix products  20 us (6%)
    pallas_call x9, Pallas kernels, exchange(): pl.pallas_call(functools.partial(exchange_kernel, axis, count, len(arrays...  165 us
    pallas_call x2, Pallas kernels, gather_with_sums(): pl.pallas_call(functools.partial(gather_kernel, axis, count, sum_axis, su...  39.8 us
    dot_general x5, matrix products, partial(): product = jnp.dot(rows, weight, preferred_element_type=jnp.float32)  13.8 us
    unnamed x34, local copies, waits for them, and re-layouts  12.2 us
    pallas_call x1, Pallas kernels, attend(): pl.pallas_call(attention_kernel, grid=(head_count, total_rows // block),...  12.1 us
    reduce_sum x6, other arithmetic, total_of(): return jnp.sum(parts.astype(jnp.float32), axis=0)  9.39 us

profile of v1, /device:TPU:15, one launch (start us, length us, event | category | flops | bytes accessed | tf_op | source)
XLA Modules:
  0.0 314.4 jit_solution(17674231454179384686)
XLA Ops:
  14.7 2.3 copy.57
  17.0 2.3 copy.58
  19.3 14.6 %shard_map.193 = bf16[4,128,1024]{2,1,0:T(8,128)(2,1)} custom-call(bf16[4,128,1024]{2,1,0:T(8,128)(2,1)} %bitcast.114), custom_call_target="tpu_custom_call" | custom-call | tf_op jit(solution)/shard_map/pallas_call | solution.py:84
  33.9 3.2 %convolution_convert_fusion.4 = bf16[512,512]{1,0:T(8,128)(2,1)} fusion(bf16[512,1024]{1,0:T(8,128)(2,1)} %bitcast.110, bf16[1024,512]{1,0:T(8,128)(2,1)} %param.21), kind=kOutput, calls=%fused_computation.9 | convolution fusion | flops 537133056 | bytes 2621440 | tf_op jit(solution)/shard_map/dot_general | solution.py:414
  40.2 19.9 %shard_map.194 = (bf16[4,128,512]{2,1,0:T(8,128)(2,1)}, bf16[4,128,512]{2,1,0:T(8,128)(2,1)}, bf16[4,128,512]{2,1,0:T(8,128)(2,1)}) custom-call(bf16[4,128,512]{2,1,0:T(8,128)(2,1)} %bitcast.132, bf16[4,128,512]{2,1,0:T(8,128)(2,1)} %bitcast.131, bf16[4,128,512]{2,1,0:T(8,128)(2,1)} %bitcast.130), custom_call_target="tpu_custom_call" | custom-call | tf_op jit(solution)/shard_map/pallas_call | solution.py:84
  60.0 2.1 convert_reduce_fusion.3
  76.6 11.3 %shard_map.195 = (bf16[4,128,512]{2,1,0:T(8,128)(2,1)}, f32[4,8,128]{2,1,0:T(8,128)}) custom-call(bf16[128,512]{1,0:T(8,128)(2,1)} %bitcast.135, f32[8,128]{1,0:T(8,128)} %get-tuple-element.52.squares_ref), custom_call_target="tpu_custom_call" | custom-call | tf_op jit(solution)/shard_map/pallas_call | solution.py:164
  95.9 12.1 %shard_map.196 = (bf16[1024,512]{1,0:T(8,128)(2,1)}, bf16[1024,512]{1,0:T(8,128)(2,1)}, bf16[512,512]{1,0:T(8,128)(2,1)S(1)}, f32[4,8,512]{2,1,0:T(8,128)S(1)}) custom-call(bf16[512,512]{1,0:T(8,128)(2,1)S(1)} %bitcast.106, f32[512,1]{1,0:T(8,128)S(1)} %copy-done.3, s32[512,1]{1,0:T(8,128)S(1)} %copy.60.old_limit_ref, s32[512,1]{1,0:T(8,128)S(1)} %copy.61.new_limit_ref, ...), custom_call_target="tpu_custom_call" | custom-call | tf_op jit(solution)/shard_map/pallas_call | solution.py:263
  109.5 9.0 %shard_map.197 = (bf16[4,128,512]{2,1,0:T(8,128)(2,1)}, f32[4,8,128]{2,1,0:T(8,128)}) custom-call(bf16[4,128,512]{2,1,0:T(8,128)(2,1)} %bitcast.107, f32[4,8,128]{2,1,0:T(8,128)} %bitcast.136), custom_call_target="tpu_custom_call" | custom-call | tf_op jit(solution)/shard_map/pallas_call | solution.py:84
  122.6 2.7 mul.240
  127.4 8.5 %shard_map.198 = bf16[4,128,512]{2,1,0:T(8,128)(2,1)} custom-call(bf16[128,512]{1,0:T(8,128)(2,1)} %multiply_reduce_fusion.refs_0_), custom_call_target="tpu_custom_call" | custom-call | tf_op jit(solution)/shard_map/pallas_call | solution.py:84
  135.9 2.1 convolution_convert_fusion.3
  139.1 26.6 %shard_map.199 = bf16[8,4,16,1024]{3,2,1,0:T(8,128)(2,1)} custom-call(bf16[8,4,16,1024]{3,2,1,0:T(8,128)(2,1)} %bitcast.115), custom_call_target="tpu_custom_call" | custom-call | tf_op jit(solution)/shard_map/pallas_call | solution.py:84
  168.5 28.5 %shard_map.200 = (bf16[8,4,16,1024]{3,2,1,0:T(8,128)(2,1)}, f32[8,8,128]{2,1,0:T(8,128)}) custom-call(bf16[4,16,1024]{2,1,0:T(8,128)(2,1)} %get-tuple-element.46.data_ref, f32[8,128]{1,0:T(8,128)} %pad.5.squares_ref), custom_call_target="tpu_custom_call" | custom-call | tf_op jit(solution)/shard_map/pallas_call | solution.py:164
  201.6 2.8 convolution_convert_fusion
  204.4 2.5 copy.68
  206.9 4.9 %convolution_convert_fusion.1 = bf16[512,1376]{0,1:T(8,128)(2,1)} fusion(bf16[512,1024]{1,0:T(8,128)(2,1)} %bitcast.123, bf16[1024,1376]{0,1:T(8,128)(2,1)} %param.26), kind=kOutput, calls=%fused_computation.1 | convolution fusion | flops 1443545088 | bytes 5275648 | tf_op jit(solution)/shard_map/dot_general | solution.py:414
  211.7 2.5 copy.67
  214.3 34.5 %shard_map.201 = (bf16[4,128,1376]{2,1,0:T(8,128)(2,1)}, bf16[4,128,1376]{2,1,0:T(8,128)(2,1)}) custom-call(bf16[4,128,1376]{2,1,0:T(8,128)(2,1)} %bitcast.109, bf16[4,128,1376]{2,1,0:T(8,128)(2,1)} %bitcast.108), custom_call_target="tpu_custom_call" | custom-call | tf_op jit(solution)/shard_map/pallas_call | solution.py:84
  251.7 18.3 %shard_map.202 = bf16[4,128,1376]{2,1,0:T(8,128)(2,1)} custom-call(bf16[128,1376]{1,0:T(8,128)(2,1)} %multiply_convert_fusion.refs_0_), custom_call_target="tpu_custom_call" | custom-call | tf_op jit(solution)/shard_map/pallas_call | solution.py:84
  270.0 4.0 %convolution_convert_fusion.2 = bf16[512,1024]{1,0:T(8,128)(2,1)S(1)} fusion(bf16[512,1376]{1,0:T(8,128)(2,1)} %bitcast.120, bf16[1376,1024]{1,0:T(8,128)(2,1)} %param.28), kind=kOutput, calls=%fused_computation.7 | convolution fusion | flops 1443364864 | bytes 5275648 | tf_op jit(solution)/shard_map/dot_general | solution.py:517
  275.1 27.1 %shard_map.203 = bf16[8,4,16,1024]{3,2,1,0:T(8,128)(2,1)} custom-call(bf16[8,4,16,1024]{3,2,1,0:T(8,128)(2,1)} %bitcast.116), custom_call_target="tpu_custom_call" | custom-call | tf_op jit(solution)/shard_map/pallas_call | solution.py:84
  302.3 2.1 reduce_sum.170.refs_0_
  304.4 6.3 %shard_map.204 = (bf16[4,16,1024]{2,1,0:T(8,128)(2,1)}, bf16[4,16,1024]{2,1,0:T(8,128)(2,1)}) custom-call(bf16[4,16,1024]{2,1,0:T(8,128)(2,1)} %reduce_sum.170.refs_0_, bf16[4,16,1024]{2,1,0:T(8,128)(2,1)} %dynamic-slice_bitcast_fusion.refs_1_), custom_call_target="tpu_custom_call" | custom-call | tf_op jit(solution)/shard_map/pallas_call | solution.py:84
  (120 shorter events, 61.2 us)
Async XLA Ops:
  0.6 201.0 %copy-start = (bf16[1024,1376]{0,1:T(8,128)(2,1)S(1)}, bf16[1024,1376]{0,1:T(8,128)(2,1)}, u32[]{:S(2)}) copy-start(bf16[1024,1376]{0,1:T(8,128)(2,1)} %param.27) | copy-start | bytes 8454148
  33.9 3.2 %copy-start.7 = (bf16[4,128,1024]{2,1,0:T(8,128)(2,1)S(1)}, bf16[4,128,1024]{2,1,0:T(8,128)(2,1)}, u32[]{:S(2)}) copy-start(bf16[4,128,1024]{2,1,0:T(8,128)(2,1)} %shard_map.193) | copy-start | bytes 3145732
  33.9 3.2 %copy-start.13 = (bf16[1024,512]{1,0:T(8,128)(2,1)S(1)}, bf16[1024,512]{1,0:T(8,128)(2,1)}, u32[]{:S(2)}) copy-start(bf16[1024,512]{1,0:T(8,128)(2,1)} %param.20) | copy-start | bytes 3145732
  37.2 1.5 copy-start.14
  62.1 0.7 copy-start.8
  90.6 1.2 copy-start.1
  91.8 1.2 copy-start.2
  93.0 0.9 copy-start.3
  94.0 1.0 copy-start.4
  95.0 0.9 copy-start.6
  108.1 0.8 copy-start.5
  122.6 2.7 copy-start.11
  139.1 58.8 %dynamic-slice-start = ((f32[4096]{0:T(1024)}, s32[]{:T(128)}), f32[1024]{0:T(1024)S(1)}, s32[]{:S(2)}) async-start(f32[4096]{0:T(1024)} %param.25, s32[]{:T(128)} %select_n.107), calls=%async_computation | async-start | bytes 8704 | tf_op jit(solution)/shard_map/dynamic_slice | solution.py:503
  200.6 1.0 copy-start.10
  248.8 1.8 copy-start.9
  302.3 11.4 %copy-start.12 = (f32[4096]{0:T(1024)S(1)}, f32[4096]{0:T(1024)}, u32[]{:S(2)}) copy-start(f32[4096]{0:T(1024)} %param.29) | copy-start | bytes 49156

commit v2 on v1

v2 whole, which is shorter than its diff:
```python
import functools
import math

import jax
import jax.numpy as jnp
from jax import lax
from jax.experimental import pallas as pl
from jax.experimental.pallas import tpu as pltpu
from jax.sharding import PartitionSpec as P

HD = 128
PLEN = 1024
SEL = 96
PPR = 2
TOKN_DEV = 32

EPSILON = 1e-06
ROPE_THETA = 500000.0
MASKED_SCORE = -1e30
MESH = pl.DeviceIdType.MESH
ANY = pl.BlockSpec(memory_space=pl.ANY)
VMEM = pl.BlockSpec(memory_space=pltpu.VMEM)


def greet(peers):
    barrier = pltpu.get_barrier_semaphore()
    for peer in peers:
        pl.semaphore_signal(barrier, inc=1, device_id=peer, device_id_type=MESH)
    pl.semaphore_wait(barrier, len(peers))


class Links:
    def __init__(self, send_sems, recv_sems, local_sems):
        self.send_sems, self.recv_sems, self.local_sems = send_sems, recv_sems, local_sems
        self.sent, self.moved = 0, 0
        self.unsent, self.started = [], []

    def send(self, source, target, peer):
        copy = pltpu.make_async_remote_copy(
            src_ref=source,
            dst_ref=target,
            send_sem=self.send_sems.at[self.sent],
            recv_sem=self.recv_sems.at[self.sent],
            device_id=peer,
            device_id_type=MESH,
        )
        copy.start()
        self.sent += 1
        self.unsent.append(copy)
        return copy

    def move(self, source, target):
        copy = pltpu.make_async_copy(source, target, self.local_sems.at[self.moved])
        copy.start()
        self.moved += 1
        return copy

    def finish(self):
        for copy in self.unsent:
            copy.wait_send()


class Pairs:
    def __init__(self, count):
        self.count, self.pairs = count, count // 2
        self.me = lax.axis_index("seq")
        self.pair, self.core = lax.div(self.me, 2), lax.rem(self.me, 2)

    def index(self, offset, other):
        core = 1 - self.core if other else self.core
        return lax.rem(self.pair + offset, self.pairs) * 2 + core

    def peer(self, offset, other):
        return {"seq": self.index(offset, other)}

    def everyone(self):
        return [
            (offset, other)
            for offset in list(range(1, self.pairs)) + [0]
            for other in (1, 0)
            if offset or other
        ]

    def source(self, offset, other):
        return ((self.pairs - offset) % self.pairs, other)


class Grid:
    def __init__(self, count):
        self.width = grid_width(count)
        self.depth = count // self.width
        self.me = lax.axis_index("blk")
        self.z, self.x = lax.div(self.me, self.width), lax.rem(self.me, self.width)

    def along_x(self, offset):
        return lax.rem(self.x + offset, self.width)

    def along_z(self, offset):
        return lax.rem(self.z + offset, self.depth)

    def x_peer(self, offset):
        return {"blk": self.z * self.width + self.along_x(offset)}

    def z_peer(self, offset):
        return {"blk": self.along_z(offset) * self.width + self.x}

    def neighbours(self):
        return [self.x_peer(o) for o in range(1, self.width)] + [
            self.z_peer(o) for o in range(1, self.depth)
        ]


def grid_width(count):
    width = 1
    while 8 * width * width <= count:
        width *= 2
    return width


def reduce_over_seq(links, seq, partial, outgoing, from_sibling, from_pairs):
    near, far = {}, []
    order = list(range(1, seq.pairs)) + [0]
    for offset in order:
        for k, piece in enumerate(partial(offset, 1)):
            outgoing[offset, 0, k] = piece.astype(jnp.bfloat16)
        near[offset] = links.send(
            outgoing.at[offset, 0], from_sibling.at[offset], seq.peer(0, 1)
        )
    for offset in order[:-1]:
        pieces = partial(offset, 0)
        near[offset].wait_recv()
        for k, piece in enumerate(pieces):
            outgoing[offset, 1, k] = (piece + from_sibling[offset, k].astype(jnp.float32)).astype(
                jnp.bfloat16
            )
        far.append(
            links.send(outgoing.at[offset, 1], from_pairs.at[offset], seq.peer(offset, 0))
        )
    totals = list(partial(0, 0))
    near[0].wait_recv()
    totals = [t + from_sibling[0, k].astype(jnp.float32) for k, t in enumerate(totals)]
    for offset, copy in zip(order[:-1], far):
        copy.wait_recv()
        totals = [t + from_pairs[offset, k].astype(jnp.float32) for k, t in enumerate(totals)]
    return totals


def share_over_seq(links, seq, buffer, use):
    mine = buffer.at[seq.me]
    far = {o: links.send(mine, mine, seq.peer(o, 0)) for o in range(1, seq.pairs)}
    near = {0: links.send(mine, mine, seq.peer(0, 1))}
    use(seq.me)
    near[0].wait_recv()
    use(seq.index(0, 1))
    for offset in range(1, seq.pairs):
        far[seq.pairs - offset].wait_recv()
        block = buffer.at[seq.index(offset, 0)]
        near[offset] = links.send(block, block, seq.peer(0, 1))
        use(seq.index(offset, 0))
    for offset in range(1, seq.pairs):
        near[offset].wait_recv()
        use(seq.index(offset, 1))


class BlockSum:
    def __init__(self, links, grid, seq, parts, from_x, summed, from_z):
        self.links, self.grid, self.seq = links, grid, seq
        self.parts, self.from_x, self.summed, self.from_z = parts, from_x, summed, from_z
        self.order, self.x_copies, self.z_copies = [], [], []

    def put(self, s, product):
        grid = self.grid
        rows = self.parts.shape[3]
        for z in range(grid.depth):
            for x in range(grid.width):
                at = (z * grid.width + x) * rows
                self.parts[s, z, x] = product[at : at + rows].astype(jnp.bfloat16)
        step = len(self.order)
        self.order.append(s)
        self.x_copies.append(
            [
                self.links.send(
                    self.parts.at[s, :, grid.along_x(o)],
                    self.from_x.at[o, step],
                    grid.x_peer(o),
                )
                for o in range(1, grid.width)
            ]
        )
        if step:
            self.pass_on(step - 1)

    def pass_on(self, step):
        grid = self.grid
        s = self.order[step]
        total = self.parts[s, :, grid.x].astype(jnp.float32)
        for o, copy in enumerate(self.x_copies[step], 1):
            copy.wait_recv()
            total += self.from_x[o, step].astype(jnp.float32)
        self.summed[step] = total.astype(jnp.bfloat16)
        self.z_copies.append(
            [
                self.links.send(
                    self.summed.at[step, grid.along_z(o)],
                    self.from_z.at[o, step],
                    grid.z_peer(o),
                )
                for o in range(1, grid.depth)
            ]
        )

    def totals(self):
        self.pass_on(len(self.order) - 1)
        for step, s in enumerate(self.order):
            total = self.summed[step, self.grid.z].astype(jnp.float32)
            for o, copy in enumerate(self.z_copies[step], 1):
                copy.wait_recv()
                total += self.from_z[o, step].astype(jnp.float32)
            yield s, total


def block_sum_scratch(seq_count, blk_count, part_rows, depth):
    width = grid_width(blk_count)
    height = blk_count // width
    return [
        pltpu.VMEM((seq_count, height, width, part_rows, depth), jnp.bfloat16),
        pltpu.VMEM((width, seq_count, height, part_rows, depth), jnp.bfloat16),
        pltpu.VMEM((seq_count, height, part_rows, depth), jnp.bfloat16),
        pltpu.VMEM((height, seq_count, part_rows, depth), jnp.bfloat16),
    ]


def semaphores(copies):
    return [
        pltpu.SemaphoreType.DMA((copies,)),
        pltpu.SemaphoreType.DMA((copies,)),
        pltpu.SemaphoreType.DMA((8,)),
    ]


def params(collective_id):
    return pltpu.CompilerParams(
        collective_id=collective_id,
        has_side_effects=True,
        vmem_limit_bytes=48 * 1024 * 1024,
    )


def columns_of(rows):
    lanes = rows.shape[1]
    return jnp.transpose(
        jnp.concatenate([rows, jnp.zeros((lanes - rows.shape[0], lanes), jnp.float32)])
    )


def project_kernel(
    seq_count,
    blk_count,
    states_ref,
    query_weight,
    key_weight,
    value_weight,
    query_gain,
    key_gain,
    cosine_ref,
    sine_ref,
    hidden_ref,
    queries_ref,
    factors_ref,
    key_rows_ref,
    value_rows_ref,
    outgoing,
    from_sibling,
    from_pairs,
    weights,
    squares,
    landing,
    sums,
    *sems,
):
    seq = Pairs(seq_count)
    row_count, depth = hidden_ref.shape[1:]
    width = key_rows_ref.shape[1]
    links = Links(*sems)
    blk = lax.axis_index("blk")
    blk_peers = [{"blk": lax.rem(blk + o, blk_count)} for o in range(1, blk_count)]
    loads = [
        links.move(ref, weights.at[k])
        for k, ref in enumerate((query_weight, key_weight, value_weight))
    ]
    own = links.move(
        states_ref.at[:, pl.ds(pl.multiple_of(seq.me * depth, depth), depth)],
        hidden_ref.at[seq.me],
    )
    greet([seq.peer(*which) for which in seq.everyone()] + blk_peers)
    arrivals = {}
    for which in seq.everyone():
        column = pl.multiple_of(seq.index(*which) * depth, depth)
        arrivals[which] = links.send(
            states_ref.at[:, pl.ds(column, depth)], hidden_ref.at[seq.me], seq.peer(*which)
        )
    for load in loads:
        load.wait()

    def partial(offset, other):
        if offset or other:
            arrivals[seq.source(offset, other)].wait_recv()
        else:
            own.wait()
        rows = hidden_ref[seq.index(offset, other)]
        return [
            jnp.dot(rows, weights[k], preferred_element_type=jnp.float32) for k in range(3)
        ]

    query, key, value = reduce_over_seq(links, seq, partial, outgoing, from_sibling, from_pairs)
    value_rows_ref[...] = value.astype(jnp.bfloat16)
    lane = lax.broadcasted_iota(jnp.int32, (row_count, HD), 1)
    query_squares = jnp.sum(query * query, axis=1, keepdims=True)
    key_squares = jnp.sum(key * key, axis=1, keepdims=True)
    squares[...] = jnp.transpose(jnp.where(lane == 0, query_squares, key_squares))[:8]
    parts = [
        links.send(squares, landing.at[o], blk_peers[o - 1]) for o in range(1, blk_count)
    ]

    def turned(raw, gain, h):
        piece = raw[:, h * HD : (h + 1) * HD] * gain[:, h * HD : (h + 1) * HD]
        return piece * cosine_ref[...] + pltpu.roll(piece, HD // 2, 1) * sine_ref[...]

    for h in range(width // HD):
        queries_ref[seq.me, :, h * HD : (h + 1) * HD] = turned(query, query_gain, h).astype(
            jnp.bfloat16
        )
    mine = queries_ref.at[seq.me]
    far = {o: links.send(mine, mine, seq.peer(o, 0)) for o in range(1, seq.pairs)}
    near = [links.send(mine, mine, seq.peer(0, 1))]
    total = squares[...]
    for o, copy in enumerate(parts, 1):
        copy.wait_recv()
        total += landing[o]
    sums[seq.me] = total
    sum_copies = [
        links.send(sums.at[seq.me], sums.at[seq.me], seq.peer(*which))
        for which in seq.everyone()
    ]
    key_factor = lax.rsqrt(columns_of(total) / (width * blk_count) + EPSILON)[:, 1:2]
    for h in range(width // HD):
        key_rows_ref[:, h * HD : (h + 1) * HD] = (turned(key, key_gain, h) * key_factor).astype(
            jnp.bfloat16
        )
    for offset in range(1, seq.pairs):
        far[seq.pairs - offset].wait_recv()
        block = queries_ref.at[seq.index(offset, 0)]
        near.append(links.send(block, block, seq.peer(0, 1)))
    for copy in sum_copies + near:
        copy.wait_recv()
    for d in range(seq_count):
        factors_ref[d] = lax.rsqrt(columns_of(sums[d]) / (width * blk_count) + EPSILON)[:, 0:1]
    links.finish()


def project(states, weights, gains, cosine, sine, seq_count, blk_count):
    row_count = states.shape[0]
    depth, width = weights[0].shape
    pairs = seq_count // 2
    bf16, f32 = jnp.bfloat16, jnp.float32
    return pl.pallas_call(
        functools.partial(project_kernel, seq_count, blk_count),
        out_shape=[
            jax.ShapeDtypeStruct((seq_count, row_count, depth), bf16),
            jax.ShapeDtypeStruct((seq_count, row_count, width), bf16),
            jax.ShapeDtypeStruct((seq_count, row_count, 1), f32),
            jax.ShapeDtypeStruct((row_count, width), bf16),
            jax.ShapeDtypeStruct((row_count, width), bf16),
        ],
        in_specs=[ANY] * 4 + [VMEM] * 4,
        out_specs=[VMEM] * 5,
        scratch_shapes=[
            pltpu.VMEM((pairs, 2, 3, row_count, width), bf16),
            pltpu.VMEM((pairs, 3, row_count, width), bf16),
            pltpu.VMEM((pairs, 3, row_count, width), bf16),
            pltpu.VMEM((3, depth, width), bf16),
            pltpu.VMEM((8, row_count), f32),
            pltpu.VMEM((blk_count, 8, row_count), f32),
            pltpu.VMEM((seq_count, 8, row_count), f32),
        ]
        + semaphores(5 * seq_count + blk_count),
        compiler_params=params(0),
    )(states, *weights, *[g.reshape(1, width) for g in gains], cosine, sine)


def mix_kernel(
    seq_count,
    blk_count,
    weighted_ref,
    stats_ref,
    weight_ref,
    hidden_ref,
    gain_ref,
    mixed_ref,
    partials,
    stats,
    attention,
    weight,
    squares,
    landing,
    parts,
    from_x,
    summed,
    from_z,
    *sems,
):
    seq, grid = Pairs(seq_count), Grid(blk_count)
    row_count, width = attention.shape[1:]
    part_rows, depth = mixed_ref.shape[2:]
    links = Links(*sems)
    load = links.move(weight_ref, weight)

    def stats_for(index):
        return stats_ref.at[:, :, pl.ds(pl.multiple_of(index * row_count, row_count), row_count)]

    own = [
        links.move(weighted_ref.at[seq.me], partials.at[seq.me]),
        links.move(stats_for(seq.me), stats.at[seq.me]),
    ]
    greet([seq.peer(*which) for which in seq.everyone()] + grid.neighbours())
    copies = []
    for which in seq.everyone():
        index = seq.index(*which)
        copies.append(links.send(stats_for(index), stats.at[seq.me], seq.peer(*which)))
        copies.append(links.send(weighted_ref.at[index], partials.at[seq.me], seq.peer(*which)))
    for copy in own:
        copy.wait()
    for copy in copies:
        copy.wait_recv()
    load.wait()
    head_count = width // HD
    shares = []
    for h in range(head_count):
        peaks = [stats[d, h, 0:1, :] for d in range(seq_count)]
        top = functools.reduce(jnp.maximum, peaks)
        scales = [jnp.exp(peak - top) for peak in peaks]
        total = sum(scale * stats[d, h, 1:2, :] for d, scale in enumerate(scales))
        shares += [scale / total for scale in scales]
    shares = columns_of(jnp.concatenate(shares))
    for h in range(head_count):
        merged = jnp.zeros((row_count, HD), jnp.float32)
        for d in range(seq_count):
            column = h * seq_count + d
            merged += (
                partials[d, :, h * HD : (h + 1) * HD].astype(jnp.float32)
                * shares[:, column : column + 1]
            )
        attention[seq.me, :, h * HD : (h + 1) * HD] = merged.astype(jnp.bfloat16)
    block_sum = BlockSum(links, grid, seq, parts, from_x, summed, from_z)

    def use(s):
        block_sum.put(
            s, jnp.dot(attention[s], weight[...], preferred_element_type=jnp.float32)
        )

    share_over_seq(links, seq, attention, use)
    for s, total in block_sum.totals():
        squares[0, s] = jnp.broadcast_to(
            jnp.sum(total * total, axis=1, keepdims=True), (part_rows, HD)
        )
        landing[s] = total
    square_copies = []
    for k, which in enumerate(seq.everyone(), 1):
        square_copies.append(links.send(squares.at[0], squares.at[k], seq.peer(*which)))
    for copy in square_copies:
        copy.wait_recv()
    factor = lax.rsqrt(jnp.sum(squares[...], axis=0) / (depth * seq_count) + EPSILON)
    update = landing[...] * factor[:, :, 0:1] * gain_ref[seq.me]
    mixed_ref[grid.me] = (
        hidden_ref[:, grid.me].astype(jnp.float32) + update
    ).astype(jnp.bfloat16)
    mine = mixed_ref.at[grid.me]
    z_copies = {o: links.send(mine, mine, grid.z_peer(o)) for o in range(1, grid.depth)}
    x_copies = [links.send(mine, mine, grid.x_peer(o)) for o in range(1, grid.width)]
    for o in range(1, grid.depth):
        z_copies[grid.depth - o].wait_recv()
        block = mixed_ref.at[grid.along_z(o) * grid.width + grid.x]
        x_copies += [links.send(block, block, grid.x_peer(x)) for x in range(1, grid.width)]
    for copy in x_copies:
        copy.wait_recv()
    links.finish()


def mix(weighted, stats, weight, hidden, gain, seq_count, blk_count):
    row_count = weighted.shape[1]
    width, depth = weight.shape
    part_rows = row_count // blk_count
    bf16, f32 = jnp.bfloat16, jnp.float32
    return pl.pallas_call(
        functools.partial(mix_kernel, seq_count, blk_count),
        out_shape=jax.ShapeDtypeStruct((blk_count, seq_count, part_rows, depth), bf16),
        in_specs=[ANY] * 3 + [VMEM] * 2,
        out_specs=VMEM,
        scratch_shapes=[
            pltpu.VMEM((seq_count, row_count, width), bf16),
            pltpu.VMEM((seq_count, width // HD, 8, row_count), f32),
            pltpu.VMEM((seq_count, row_count, width), bf16),
            pltpu.VMEM((width, depth), bf16),
            pltpu.VMEM((seq_count, seq_count, part_rows, HD), f32),
            pltpu.VMEM((seq_count, part_rows, depth), f32),
        ]
        + block_sum_scratch(seq_count, blk_count, part_rows, depth)
        + semaphores(4 * seq_count + (seq_count + 3) * blk_count),
        compiler_params=params(1),
    )(
        weighted,
        stats,
        weight,
        hidden.reshape(seq_count, blk_count, part_rows, depth),
        gain.reshape(seq_count, 1, depth),
    )


def feed_kernel(
    seq_count,
    blk_count,
    gate_ref,
    up_ref,
    down_ref,
    mixed_ref,
    gain_ref,
    out_ref,
    gate_up,
    down,
    outgoing,
    from_sibling,
    from_pairs,
    activation,
    halves,
    mixed_parts,
    final_parts,
    parts,
    from_x,
    summed,
    from_z,
    *sems,
):
    seq, grid = Pairs(seq_count), Grid(blk_count)
    part_rows, depth = mixed_ref.shape[2:]
    links = Links(*sems)
    loads = [links.move(gate_ref, gate_up.at[0]), links.move(up_ref, gate_up.at[1])]
    down_load = links.move(down_ref, down)
    greet([seq.peer(*which) for which in seq.everyone()] + grid.neighbours())
    mixed_copies = [
        links.send(
            mixed_ref.at[grid.me, seq.index(*which)], mixed_parts.at[seq.me], seq.peer(*which)
        )
        for which in seq.everyone()
    ]
    mixed_parts[seq.me] = mixed_ref[grid.me, seq.me]
    for load in loads:
        load.wait()

    def partial(offset, other):
        rows = mixed_ref[:, seq.index(offset, other)].astype(jnp.float32)
        rows = rows.reshape(blk_count * part_rows, depth).astype(jnp.bfloat16)
        return [
            lax.dot_general(
                rows, gate_up[k], (((1,), (1,)), ((), ())), preferred_element_type=jnp.float32
            )
            for k in range(2)
        ]

    gate, up = reduce_over_seq(links, seq, partial, outgoing, from_sibling, from_pairs)
    activation[seq.me] = (gate / (1.0 + jnp.exp(-gate)) * up).astype(jnp.bfloat16)
    down_load.wait()
    block_sum = BlockSum(links, grid, seq, parts, from_x, summed, from_z)

    def use(s):
        block_sum.put(
            s, jnp.dot(activation[s], down[...], preferred_element_type=jnp.float32)
        )

    share_over_seq(links, seq, activation, use)
    for s, total in block_sum.totals():
        halves[s] = total.astype(jnp.bfloat16)
    final_parts[seq.me] = halves[seq.me]
    final_copies = [
        links.send(halves.at[seq.index(*which)], final_parts.at[seq.me], seq.peer(*which))
        for which in seq.everyone()
    ]
    for copy in mixed_copies + final_copies:
        copy.wait_recv()
    pieces = [final_parts[d].astype(jnp.float32) for d in range(seq_count)]
    squares = sum(jnp.sum(piece * piece, axis=1, keepdims=True) for piece in pieces)
    factor = lax.rsqrt(squares / (depth * seq_count) + EPSILON)
    for d, piece in enumerate(pieces):
        columns = slice(d * depth, (d + 1) * depth)
        out_ref[:, columns] = (
            mixed_parts[d].astype(jnp.float32) + piece * factor * gain_ref[:, columns]
        ).astype(jnp.bfloat16)
    links.finish()


def feed(gate, up, down, mixed, gain, seq_count, blk_count):
    units, depth = gate.shape
    part_rows = mixed.shape[2]
    row_count = part_rows * blk_count
    pairs = seq_count // 2
    bf16 = jnp.bfloat16
    return pl.pallas_call(
        functools.partial(feed_kernel, seq_count, blk_count),
        out_shape=jax.ShapeDtypeStruct((part_rows, depth * seq_count), bf16),
        in_specs=[ANY] * 3 + [VMEM] * 2,
        out_specs=VMEM,
        scratch_shapes=[
            pltpu.VMEM((2, units, depth), bf16),
            pltpu.VMEM((units, depth), bf16),
            pltpu.VMEM((pairs, 2, 2, row_count, units), bf16),
            pltpu.VMEM((pairs, 2, row_count, units), bf16),
            pltpu.VMEM((pairs, 2, row_count, units), bf16),
            pltpu.VMEM((seq_count, row_count, units), bf16),
            pltpu.VMEM((seq_count, part_rows, depth), bf16),
            pltpu.VMEM((seq_count, part_rows, depth), bf16),
            pltpu.VMEM((seq_count, part_rows, depth), bf16),
        ]
        + block_sum_scratch(seq_count, blk_count, part_rows, depth)
        + semaphores(5 * seq_count + seq_count * blk_count),
        compiler_params=params(2),
    )(gate, up, down, mixed, gain.reshape(1, -1))


def attention_kernel(
    query_ref,
    factor_ref,
    old_limit_ref,
    new_limit_ref,
    picked_ref,
    turn_ref,
    old_keys_ref,
    old_values_ref,
    key_rows_ref,
    value_rows_ref,
    keys_ref,
    values_ref,
    weighted_ref,
    stats_ref,
):
    @pl.when(pl.program_id(1) == 0)
    def blend():
        row_count = key_rows_ref.shape[0]
        token = lax.broadcasted_iota(jnp.int32, (PLEN, row_count), 0)
        hit = token == picked_ref[...]
        chosen = jnp.where(hit, 1.0, 0.0)
        replaced = jnp.max(chosen, axis=1, keepdims=True) > 0.5
        chosen = chosen.astype(jnp.bfloat16)
        old = old_keys_ref[...].astype(jnp.float32)
        turned = old * turn_ref[0:1, :] + pltpu.roll(old, HD // 2, 1) * turn_ref[1:2, :]
        new_keys = jnp.dot(chosen, key_rows_ref[...], preferred_element_type=jnp.float32)
        keys_ref[...] = jnp.where(replaced, new_keys, turned).astype(jnp.bfloat16)
        new_values = jnp.dot(chosen, value_rows_ref[...], preferred_element_type=jnp.float32)
        values_ref[...] = jnp.where(
            replaced, new_values, old_values_ref[...].astype(jnp.float32)
        ).astype(jnp.bfloat16)

    query = (query_ref[...].astype(jnp.float32) * factor_ref[...]).astype(jnp.bfloat16)
    contract = (((1,), (1,)), ((), ()))
    old_scores = lax.dot_general(
        query, keys_ref[...], contract, preferred_element_type=jnp.float32
    )
    new_scores = lax.dot_general(
        query, key_rows_ref[...], contract, preferred_element_type=jnp.float32
    )
    scale = HD ** (-0.5)
    old_seen = lax.broadcasted_iota(jnp.int32, old_scores.shape, 1) <= old_limit_ref[...]
    new_token = lax.broadcasted_iota(jnp.int32, new_scores.shape, 1) - SEL
    new_seen = (new_token >= 0) & (new_token <= new_limit_ref[...])
    old_scores = jnp.where(old_seen, old_scores * scale, MASKED_SCORE)
    new_scores = jnp.where(new_seen, new_scores * scale, MASKED_SCORE)
    peak = jnp.maximum(
        jnp.max(old_scores, axis=1, keepdims=True), jnp.max(new_scores, axis=1, keepdims=True)
    )
    old_weights = jnp.where(old_seen, jnp.exp(old_scores - peak), 0.0)
    new_weights = jnp.where(new_seen, jnp.exp(new_scores - peak), 0.0)
    total = jnp.sum(old_weights, axis=1, keepdims=True) + jnp.sum(
        new_weights, axis=1, keepdims=True
    )
    weighted = jnp.dot(
        old_weights.astype(jnp.bfloat16), values_ref[...], preferred_element_type=jnp.float32
    ) + jnp.dot(
        new_weights.astype(jnp.bfloat16), value_rows_ref[...], preferred_element_type=jnp.float32
    )
    weighted_ref[...] = weighted.astype(jnp.bfloat16)
    lane = lax.broadcasted_iota(jnp.int32, weighted.shape, 1)
    stats = jnp.transpose(jnp.where(lane == 0, peak, total))
    stats_ref[0] = stats[:8, :]


def attend(
    queries, factor, old_limit, new_limit, picked, turn, old_keys, old_values, key_rows, value_rows
):
    total_rows, width = queries.shape
    row_count = key_rows.shape[0]
    head_count = width // HD
    block = min(total_rows, 512)
    by_row = pl.BlockSpec((block, 1), lambda h, i: (i, 0))
    by_head = pl.BlockSpec((PLEN, HD), lambda h, i: (0, h))
    rows_by_head = pl.BlockSpec((row_count, HD), lambda h, i: (0, h))
    tile = pl.BlockSpec((block, HD), lambda h, i: (i, h))
    return pl.pallas_call(
        attention_kernel,
        grid=(head_count, total_rows // block),
        out_shape=[
            jax.ShapeDtypeStruct((PLEN, width), jnp.bfloat16),
            jax.ShapeDtypeStruct((PLEN, width), jnp.bfloat16),
            jax.ShapeDtypeStruct((total_rows, width), jnp.bfloat16),
            jax.ShapeDtypeStruct((head_count, 8, total_rows), jnp.float32),
        ],
        in_specs=[
            tile,
            by_row,
            by_row,
            by_row,
            pl.BlockSpec((1, row_count), lambda h, i: (0, 0)),
            pl.BlockSpec((8, HD), lambda h, i: (0, 0)),
            by_head,
            by_head,
            rows_by_head,
            rows_by_head,
        ],
        out_specs=[
            by_head,
            by_head,
            tile,
            pl.BlockSpec((1, 8, block), lambda h, i: (h, 0, i)),
        ],
        compiler_params=pltpu.CompilerParams(vmem_limit_bytes=48 * 1024 * 1024),
    )(
        queries,
        factor,
        old_limit,
        new_limit,
        picked,
        turn,
        old_keys,
        old_values,
        key_rows,
        value_rows,
    )


def frequencies():
    indices = jnp.arange(HD // 2, dtype=jnp.float32)
    return jnp.exp(indices * (-2.0 * math.log(ROPE_THETA) / HD))


def layout(passage_order, separators, recompute_index, seq_count):
    devices = jnp.arange(seq_count, dtype=jnp.int32)
    slots = jnp.arange(PPR, dtype=jnp.int32)
    earlier = slots[None, :, None] >= slots[None, None, :]
    opening = slots[None, :] * PLEN + jnp.sum(
        jnp.where(earlier, separators[:, None, :], 0), axis=2
    )
    hit = passage_order[None, :] == devices[:, None]
    starts = jnp.sum(jnp.where(hit, opening.reshape(-1)[None, :], 0), axis=1)
    owners = jnp.sum(jnp.where(hit, (devices // PPR)[None, :], 0), axis=1)
    prompt_start = jnp.repeat(opening[:, PPR - 1] + PLEN, PPR)
    offsets = (devices % PPR) * TOKN_DEV
    new_starts = prompt_start + offsets
    new_positions = new_starts[:, None] + jnp.arange(TOKN_DEV, dtype=jnp.int32)[None, :]
    positions = jnp.concatenate([starts[:, None] + recompute_index, new_positions], axis=1)
    requests = jnp.concatenate(
        [
            jnp.broadcast_to(owners[:, None], recompute_index.shape),
            jnp.broadcast_to((devices // PPR)[:, None], new_positions.shape),
        ],
        axis=1,
    )
    return starts, owners, new_starts, offsets, positions, requests


def shards(
    hidden_states,
    query_weight,
    key_weight,
    value_weight,
    output_weight,
    query_gain,
    key_gain,
    attention_gain,
    gate_weight,
    up_weight,
    down_weight,
    feedforward_gain,
    cached_keys,
    cached_values,
    passage_order,
    separators,
    recompute_index,
    prompt_lengths,
):
    seq_count = lax.axis_size("seq")
    blk_count = lax.axis_size("blk")
    seq_index = lax.axis_index("seq")
    row_count = hidden_states.shape[0]
    local_width = query_weight.shape[1]
    total_rows = row_count * seq_count

    def mine(array):
        return lax.dynamic_index_in_dim(array, seq_index, 0, keepdims=False)

    starts, owners, new_starts, offsets, positions, requests = layout(
        passage_order, separators, recompute_index, seq_count
    )
    frequency = frequencies()
    passage_start = mine(starts)
    own_request = seq_index // PPR
    old_limit = jnp.where(requests == mine(owners), positions - passage_start, -1)
    live_limit = lax.dynamic_index_in_dim(prompt_lengths, own_request, 0, False) - 1 - mine(offsets)
    new_limit = jnp.where(
        requests == own_request, jnp.minimum(positions - mine(new_starts), live_limit), -1
    )
    picked = jnp.concatenate(
        [mine(recompute_index), jnp.full((row_count - SEL,), -1, jnp.int32)]
    ).reshape(1, row_count)
    turn_angles = passage_start.astype(jnp.float32) * frequency
    turn_cosine, turn_sine = jnp.cos(turn_angles), jnp.sin(turn_angles)
    turn = jnp.concatenate(
        [
            jnp.concatenate([turn_cosine, turn_cosine])[None],
            jnp.concatenate([-turn_sine, turn_sine])[None],
            jnp.zeros((6, HD), jnp.float32),
        ]
    )
    angles = mine(positions).astype(jnp.float32)[:, None] * frequency[None, :]
    cosine, sine = jnp.cos(angles), jnp.sin(angles)
    hidden, queries, factors, key_rows, value_rows = project(
        hidden_states,
        (query_weight, key_weight, value_weight),
        (query_gain, key_gain),
        jnp.concatenate([cosine, cosine], axis=1),
        jnp.concatenate([-sine, sine], axis=1),
        seq_count,
        blk_count,
    )
    passage_keys, passage_values, weighted, stats = attend(
        queries.reshape(total_rows, local_width),
        factors.reshape(total_rows, 1),
        old_limit.reshape(total_rows, 1),
        new_limit.reshape(total_rows, 1),
        picked,
        turn,
        cached_keys[0],
        cached_values[0],
        key_rows,
        value_rows,
    )
    mixed = mix(
        weighted.reshape(seq_count, row_count, local_width),
        stats,
        output_weight,
        hidden,
        attention_gain,
        seq_count,
        blk_count,
    )
    hidden_out = feed(
        gate_weight.T, up_weight.T, down_weight, mixed, feedforward_gain, seq_count, blk_count
    )
    return (hidden_out, passage_keys[None], passage_values[None])


def solution(mesh):
    return jax.shard_map(
        shards,
        mesh=mesh,
        in_specs=(
            P("seq", None),
            P("seq", "blk"),
            P("seq", "blk"),
            P("seq", "blk"),
            P("blk", "seq"),
            P("blk"),
            P("blk"),
            P(),
            P("seq", "blk"),
            P("seq", "blk"),
            P("blk", "seq"),
            P(),
            P("seq", None, "blk"),
            P("seq", None, "blk"),
            P(),
            P(),
            P(),
            P(),
        ),
        out_specs=(P(("seq", "blk"), None), P("seq", None, "blk"), P("seq", None, "blk")),
        check_vma=False,
    )
```

time: 316 us -> 173 us (0.55)
  the two profiles are of different devices: /device:TPU:15 before, /device:TPU:0 now
where the time goes in v2:
time: 173 us
  Pallas kernels  154 us (89%)
  local copies, waits for them, and re-layouts  10.8 us (6%)
  other arithmetic  5.52 us (3%)
  between operations  2.82 us (2%)
    pallas_call x1, Pallas kernels, feed(): pl.pallas_call(functools.partial(feed_kernel, seq_count, blk_count), out_...  54.4 us
    pallas_call x1, Pallas kernels, mix(): pl.pallas_call(functools.partial(mix_kernel, seq_count, blk_count), out_s...  51 us
    pallas_call x1, Pallas kernels, project(): pl.pallas_call(functools.partial(project_kernel, seq_count, blk_count), o...  36.2 us
    pallas_call x1, Pallas kernels, attend(): pl.pallas_call(attention_kernel, grid=(head_count, total_rows // block),...  12.1 us
    unnamed x23, local copies, waits for them, and re-layouts  5.73 us

profile of v2, /device:TPU:0, one launch (start us, length us, event | category | flops | bytes accessed | tf_op | source)
XLA Modules:
  0.0 172.9 jit_solution(4762980260050605936)
XLA Ops:
  0.7 1.3 dynamic_slice.29
  2.6 0.7 dynamic-slice_bitcast_fusion
  3.4 0.8 select_reduce_fusion.2
  4.3 0.2 add_reduce_fusion
  4.7 0.6 dynamic_slice.28
  5.3 0.6 dynamic_slice.30
  6.5 0.8 select_reduce_fusion
  7.3 0.6 dynamic_slice.27
  8.6 0.6 dynamic_slice.26
  9.7 0.8 broadcast_add_fusion
  10.5 0.7 minimum_select_fusion
  11.2 1.3 subtract_select_fusion
  12.5 0.3 fusion
  13.2 0.1 copy.28.new_limit_ref
  13.4 1.2 copy-done.1
  14.6 1.2 copy-done.2
  15.8 1.2 copy-done.3
  17.0 0.7 copy-done.9
  17.7 0.7 copy-done.10
  18.4 36.2 %shard_map.193 = (bf16[4,128,1024]{2,1,0:T(8,128)(2,1)S(1)}, bf16[4,128,512]{2,1,0:T(8,128)(2,1)S(1)}, f32[4,128,1]{2,1,0:T(8,128)S(1)}, bf16[128,512]{1,0:T(8,128)(2,1)S(1)}, bf16[128,512]{1,0:T(8,128)(2,1)S(1)}) custom-call(bf16[128,4096]{1,0:T(8,128)(2,1)S(1)} %copy-done.1, bf16[1024,512]{1,0:T(8,128)(2,1)S(1)} %copy-done.2, ...), custom_call_target="tpu_custom_call" | custom-call | tf_op jit(solution)/shard_map/pallas_call | solution.py:366
  54.7 12.1 %shard_map.194 = (bf16[1024,512]{1,0:T(8,128)(2,1)}, bf16[1024,512]{1,0:T(8,128)(2,1)}, bf16[512,512]{1,0:T(8,128)(2,1)S(1)}, f32[4,8,512]{2,1,0:T(8,128)S(1)}) custom-call(bf16[512,512]{1,0:T(8,128)(2,1)S(1)} %bitcast.34, f32[512,1]{1,0:T(8,128)S(1)} %bitcast.36, s32[512,1]{1,0:T(8,128)S(1)} %copy.27.old_limit_ref, s32[512,1]{1,0:T(8,128)S(1)} %copy.28.new_limit_ref, ...), custom_call_target="tpu_custom_call" | custom-call | tf_op jit(solution)/shard_map/pallas_call | solution.py:705
  66.8 51.0 %shard_map.195.mixed_ref = bf16[8,4,16,1024]{3,2,1,0:T(8,128)(2,1)S(1)} custom-call(bf16[4,128,512]{2,1,0:T(8,128)(2,1)S(1)} %bitcast.35, f32[4,8,512]{2,1,0:T(8,128)S(1)} %get-tuple-element.17.stats_ref, bf16[512,1024]{1,0:T(8,128)(2,1)S(1)} %copy-done.6, bf16[4,8,16,1024]{3,2,1,0:T(8,128)(2,1)S(1)} %bitcast.33, f32[4,1,1024]{2,1,0:T(1,128)S(1)} %bitcast.37), custom_call_target="tpu_custom_call" | custom-call | tf_op jit(solution)/shard_map/pallas_call | solution.py:494
  117.8 54.4 %shard_map.196 = bf16[16,4096]{1,0:T(8,128)(2,1)S(1)} custom-call(bf16[1376,1024]{1,0:T(8,128)(2,1)S(1)} %bitcast.30, bf16[1376,1024]{1,0:T(8,128)(2,1)} %bitcast.41, bf16[1376,1024]{1,0:T(8,128)(2,1)} %down_ref.1, bf16[8,4,16,1024]{3,2,1,0:T(8,128)(2,1)S(1)} %shard_map.195.mixed_ref, f32[1,4096]{1,0:T(1,128)S(1)} %bitcast.38), custom_call_target="tpu_custom_call" | custom-call | tf_op jit(solution)/shard_map/pallas_call | solution.py:606
  172.2 0.7 copy.30
  (42 shorter events, 1.3 us)
Async XLA Ops:
  0.6 54.0 %copy-start.4 = (bf16[1,1024,512]{2,1,0:T(8,128)(2,1)S(1)}, bf16[1,1024,512]{2,1,0:T(8,128)(2,1)}, u32[]{:S(2)}) copy-start(bf16[1,1024,512]{2,1,0:T(8,128)(2,1)} %param.30) | copy-start | bytes 3145732
  13.3 1.2 copy-start.1
  14.6 1.2 copy-start.2
  15.8 1.2 copy-start.3
  17.0 0.7 copy-start.9
  17.7 0.7 copy-start.10
  18.4 36.2 %copy-start.5 = (bf16[1,1024,512]{2,1,0:T(8,128)(2,1)S(1)}, bf16[1,1024,512]{2,1,0:T(8,128)(2,1)}, u32[]{:S(2)}) copy-start(bf16[1,1024,512]{2,1,0:T(8,128)(2,1)} %param.31) | copy-start | bytes 3145732
  54.6 12.2 %copy-start.6 = (bf16[512,1024]{1,0:T(8,128)(2,1)S(1)}, bf16[512,1024]{1,0:T(8,128)(2,1)}, u32[]{:S(2)}) copy-start(bf16[512,1024]{1,0:T(8,128)(2,1)} %weight_ref.1) | copy-start | bytes 3145732
  54.6 12.2 %copy-start.7 = (f32[4096]{0:T(1024)S(1)}, f32[4096]{0:T(1024)}, u32[]{:S(2)}) copy-start(f32[4096]{0:T(1024)} %param.25) | copy-start | bytes 49156
  54.6 63.1 %copy-start = (bf16[1024,1376]{0,1:T(8,128)(2,1)S(1)}, bf16[1024,1376]{0,1:T(8,128)(2,1)}, u32[]{:S(2)}) copy-start(bf16[1024,1376]{0,1:T(8,128)(2,1)} %param.26) | copy-start | bytes 8454148
  54.7 63.1 %copy-start.8 = (f32[4096]{0:T(1024)S(1)}, f32[4096]{0:T(1024)}, u32[]{:S(2)}) copy-start(f32[4096]{0:T(1024)} %param.29) | copy-start | bytes 49156

commit v3 on v2

--- a/solution.py
+++ b/solution.py
@@ -238,11 +238,11 @@
     ]
 
 
-def params(collective_id):
+def params(collective_id, mebibytes):
     return pltpu.CompilerParams(
         collective_id=collective_id,
         has_side_effects=True,
-        vmem_limit_bytes=48 * 1024 * 1024,
+        vmem_limit_bytes=mebibytes * 1024 * 1024,
     )
 
 
@@ -384,19 +384,23 @@
             pltpu.VMEM((seq_count, 8, row_count), f32),
         ]
         + semaphores(5 * seq_count + blk_count),
-        compiler_params=params(0),
+        compiler_params=params(0, 60),
     )(states, *weights, *[g.reshape(1, width) for g in gains], cosine, sine)
 
 
-def mix_kernel(
+def finish_kernel(
     seq_count,
     blk_count,
     weighted_ref,
     stats_ref,
     weight_ref,
+    gate_ref,
+    up_ref,
+    down_ref,
     hidden_ref,
-    gain_ref,
-    mixed_ref,
+    attention_gain,
+    feed_gain,
+    out_ref,
     partials,
     stats,
     attention,
@@ -407,13 +411,29 @@
     from_x,
     summed,
     from_z,
+    gate_up,
+    down,
+    mixed,
+    mixed_parts,
+    final_parts,
+    halves,
+    outgoing,
+    from_sibling,
+    from_pairs,
+    activation,
+    feed_parts,
+    feed_from_x,
+    feed_summed,
+    feed_from_z,
     *sems,
 ):
     seq, grid = Pairs(seq_count), Grid(blk_count)
     row_count, width = attention.shape[1:]
-    part_rows, depth = mixed_ref.shape[2:]
+    part_rows, depth = mixed.shape[3:]
     links = Links(*sems)
     load = links.move(weight_ref, weight)
+    gate_loads = [links.move(gate_ref, gate_up.at[0]), links.move(up_ref, gate_up.at[1])]
+    down_load = links.move(down_ref, down)
 
     def stats_for(index):
         return stats_ref.at[:, :, pl.ds(pl.multiple_of(index * row_count, row_count), row_count)]
@@ -470,31 +490,158 @@
     for copy in square_copies:
         copy.wait_recv()
     factor = lax.rsqrt(jnp.sum(squares[...], axis=0) / (depth * seq_count) + EPSILON)
-    update = landing[...] * factor[:, :, 0:1] * gain_ref[seq.me]
-    mixed_ref[grid.me] = (
-        hidden_ref[:, grid.me].astype(jnp.float32) + update
-    ).astype(jnp.bfloat16)
-    mine = mixed_ref.at[grid.me]
-    z_copies = {o: links.send(mine, mine, grid.z_peer(o)) for o in range(1, grid.depth)}
-    x_copies = [links.send(mine, mine, grid.x_peer(o)) for o in range(1, grid.width)]
-    for o in range(1, grid.depth):
-        z_copies[grid.depth - o].wait_recv()
-        block = mixed_ref.at[grid.along_z(o) * grid.width + grid.x]
-        x_copies += [links.send(block, block, grid.x_peer(x)) for x in range(1, grid.width)]
-    for copy in x_copies:
+    update = landing[...] * factor[:, :, 0:1] * attention_gain[seq.me]
+    mixed[grid.z, grid.x] = (hidden_ref[:, grid.me].astype(jnp.float32) + update).astype(
+        jnp.bfloat16
+    )
+
+    chunks = grid.depth
+    order = list(range(1, seq.pairs)) + [0]
+    mine = mixed.at[grid.z, grid.x]
+    x_copies = {0: [links.send(mine, mine, grid.x_peer(o)) for o in range(1, grid.width)]}
+    z_copies = {c: links.send(mine, mine, grid.z_peer(chunks - c)) for c in range(1, chunks)}
+    mixed_copies = [
+        links.send(mixed.at[grid.z, grid.x, seq.index(*which)], mixed_parts.at[seq.me], peer)
+        for which, peer in [(which, seq.peer(*which)) for which in seq.everyone()]
+    ]
+    mixed_parts[seq.me] = mixed[grid.z, grid.x, seq.me]
+    for gate_load in gate_loads:
+        gate_load.wait()
+    down_load.wait()
+    near, far, act_far, act_near, part_copies, sum_copies = {}, {}, {}, {}, {}, {}
+
+    def pass_mixed(c):
+        z_copies[c].wait_recv()
+        block = mixed.at[grid.along_z(c), grid.x]
+        x_copies[c] = [links.send(block, block, grid.x_peer(o)) for o in range(1, grid.width)]
+
+    def multiply_gate_up(c):
+        for copy in x_copies[c]:
+            copy.wait_recv()
+        rows = mixed[grid.along_z(c)].astype(jnp.float32)
+        rows = rows.reshape(grid.width * seq_count * part_rows, depth).astype(jnp.bfloat16)
+        for k in range(2):
+            product = lax.dot_general(
+                rows, gate_up[k], (((1,), (1,)), ((), ())), preferred_element_type=jnp.float32
+            ).astype(jnp.bfloat16)
+            for x in range(grid.width):
+                for s in range(seq_count):
+                    at = (x * seq_count + s) * part_rows
+                    outgoing[c, s, k, x] = product[at : at + part_rows]
+        for offset in order:
+            near[c, offset] = links.send(
+                outgoing.at[c, seq.index(offset, 1)],
+                from_sibling.at[c, offset],
+                seq.peer(0, 1),
+            )
+
+    def sum_of_pair(c, offset):
+        near[c, offset].wait_recv()
+        return outgoing[c, seq.index(offset, 0)].astype(jnp.float32) + from_sibling[
+            c, offset
+        ].astype(jnp.float32)
+
+    def send_pair_sums(c):
+        for offset in order[:-1]:
+            outgoing[c, seq.index(offset, 0)] = sum_of_pair(c, offset).astype(jnp.bfloat16)
+            far[c, offset] = links.send(
+                outgoing.at[c, seq.index(offset, 0)],
+                from_pairs.at[c, offset],
+                seq.peer(offset, 0),
+            )
+
+    def activate(c):
+        total = sum_of_pair(c, 0)
+        for offset in order[:-1]:
+            far[c, offset].wait_recv()
+            total += from_pairs[c, offset].astype(jnp.float32)
+        gate, up = total[0], total[1]
+        activation[c, seq.me] = (gate / (1.0 + jnp.exp(-gate)) * up).astype(jnp.bfloat16)
+        block = activation.at[c, seq.me]
+        for offset in order[:-1]:
+            act_far[c, offset] = links.send(block, block, seq.peer(offset, 0))
+        act_near[c] = [links.send(block, block, seq.peer(0, 1))]
+
+    def multiply_down(c):
+        for offset in order[:-1]:
+            act_far[c, seq.pairs - offset].wait_recv()
+            block = activation.at[c, seq.index(offset, 0)]
+            act_near[c].append(links.send(block, block, seq.peer(0, 1)))
+        for copy in act_near[c]:
+            copy.wait_recv()
+        rows = activation[c].astype(jnp.float32)
+        rows = rows.reshape(seq_count * grid.width * part_rows, rows.shape[-1])
+        product = jnp.dot(
+            rows.astype(jnp.bfloat16), down[...], preferred_element_type=jnp.float32
+        ).astype(jnp.bfloat16)
+        for s in range(seq_count):
+            for x in range(grid.width):
+                at = (s * grid.width + x) * part_rows
+                feed_parts[c, x, s] = product[at : at + part_rows]
+        part_copies[c] = [
+            links.send(
+                feed_parts.at[c, grid.along_x(o)], feed_from_x.at[c, o], grid.x_peer(o)
+            )
+            for o in range(1, grid.width)
+        ]
+
+    def sum_over_x(c):
+        total = feed_parts[c, grid.x].astype(jnp.float32)
+        for o, copy in enumerate(part_copies[c], 1):
+            copy.wait_recv()
+            total += feed_from_x[c, o].astype(jnp.float32)
+        feed_summed[c] = total.astype(jnp.bfloat16)
+        if c:
+            sum_copies[c] = links.send(feed_summed.at[c], feed_from_z.at[c], grid.z_peer(c))
+
+    for step in range(chunks + 3):
+        if step < chunks:
+            multiply_gate_up(step)
+            if step + 1 < chunks:
+                pass_mixed(step + 1)
+            send_pair_sums(step)
+        if 0 <= step - 1 < chunks:
+            activate(step - 1)
+        if 0 <= step - 2 < chunks:
+            multiply_down(step - 2)
+        if 0 <= step - 3 < chunks:
+            sum_over_x(step - 3)
+    total = feed_summed[0].astype(jnp.float32)
+    for c in range(1, chunks):
+        sum_copies[c].wait_recv()
+        total += feed_from_z[c].astype(jnp.float32)
+    halves[...] = total.astype(jnp.bfloat16)
+    final_parts[seq.me] = halves[seq.me]
+    final_copies = [
+        links.send(halves.at[seq.index(*which)], final_parts.at[seq.me], seq.peer(*which))
+        for which in seq.everyone()
+    ]
+    for copy in mixed_copies + final_copies:
         copy.wait_recv()
+    pieces = [final_parts[d].astype(jnp.float32) for d in range(seq_count)]
+    squares_total = sum(jnp.sum(piece * piece, axis=1, keepdims=True) for piece in pieces)
+    factor = lax.rsqrt(squares_total / (depth * seq_count) + EPSILON)
+    for d, piece in enumerate(pieces):
+        columns = slice(d * depth, (d + 1) * depth)
+        out_ref[:, columns] = (
+            mixed_parts[d].astype(jnp.float32) + piece * factor * feed_gain[:, columns]
+        ).astype(jnp.bfloat16)
     links.finish()
 
 
-def mix(weighted, stats, weight, hidden, gain, seq_count, blk_count):
+def finish(weighted, stats, weights, hidden, gains, seq_count, blk_count):
     row_count = weighted.shape[1]
-    width, depth = weight.shape
+    width, depth = weights[0].shape
+    units = weights[1].shape[0]
     part_rows = row_count // blk_count
+    pairs = seq_count // 2
+    across = grid_width(blk_count)
+    chunks = blk_count // across
     bf16, f32 = jnp.bfloat16, jnp.float32
     return pl.pallas_call(
-        functools.partial(mix_kernel, seq_count, blk_count),
-        out_shape=jax.ShapeDtypeStruct((blk_count, seq_count, part_rows, depth), bf16),
-        in_specs=[ANY] * 3 + [VMEM] * 2,
+        functools.partial(finish_kernel, seq_count, blk_count),
+        out_shape=jax.ShapeDtypeStruct((part_rows, depth * seq_count), bf16),
+        in_specs=[ANY] * 6 + [VMEM] * 3,
         out_specs=VMEM,
         scratch_shapes=[
             pltpu.VMEM((seq_count, row_count, width), bf16),
@@ -505,124 +652,32 @@
             pltpu.VMEM((seq_count, part_rows, depth), f32),
         ]
         + block_sum_scratch(seq_count, blk_count, part_rows, depth)
-        + semaphores(4 * seq_count + (seq_count + 3) * blk_count),
-        compiler_params=params(1),
+        + [
+            pltpu.VMEM((2, units, depth), bf16),
+            pltpu.VMEM((units, depth), bf16),
+            pltpu.VMEM((chunks, across, seq_count, part_rows, depth), bf16),
+            pltpu.VMEM((seq_count, part_rows, depth), bf16),
+            pltpu.VMEM((seq_count, part_rows, depth), bf16),
+            pltpu.VMEM((seq_count, part_rows, depth), bf16),
+            pltpu.VMEM((chunks, seq_count, 2, across, part_rows, units), bf16),
+            pltpu.VMEM((chunks, pairs, 2, across, part_rows, units), bf16),
+            pltpu.VMEM((chunks, pairs, 2, across, part_rows, units), bf16),
+            pltpu.VMEM((chunks, seq_count, across, part_rows, units), bf16),
+            pltpu.VMEM((chunks, across, seq_count, part_rows, depth), bf16),
+            pltpu.VMEM((chunks, across, seq_count, part_rows, depth), bf16),
+            pltpu.VMEM((chunks, seq_count, part_rows, depth), bf16),
+            pltpu.VMEM((chunks, seq_count, part_rows, depth), bf16),
+        ]
+        + semaphores(8 * seq_count + (2 * seq_count + 3) * blk_count),
+        compiler_params=params(1, 48),
     )(
         weighted,
         stats,
-        weight,
+        *weights,
         hidden.reshape(seq_count, blk_count, part_rows, depth),
-        gain.reshape(seq_count, 1, depth),
-    )
-
-
-def feed_kernel(
-    seq_count,
-    blk_count,
-    gate_ref,
-    up_ref,
-    down_ref,
-    mixed_ref,
-    gain_ref,
-    out_ref,
-    gate_up,
-    down,
-    outgoing,
-    from_sibling,
-    from_pairs,
-    activation,
-    halves,
-    mixed_parts,
-    final_parts,
-    parts,
-    from_x,
-    summed,
-    from_z,
-    *sems,
-):
-    seq, grid = Pairs(seq_count), Grid(blk_count)
-    part_rows, depth = mixed_ref.shape[2:]
-    links = Links(*sems)
-    loads = [links.move(gate_ref, gate_up.at[0]), links.move(up_ref, gate_up.at[1])]
-    down_load = links.move(down_ref, down)
-    greet([seq.peer(*which) for which in seq.everyone()] + grid.neighbours())
-    mixed_copies = [
-        links.send(
-            mixed_ref.at[grid.me, seq.index(*which)], mixed_parts.at[seq.me], seq.peer(*which)
-        )
-        for which in seq.everyone()
-    ]
-    mixed_parts[seq.me] = mixed_ref[grid.me, seq.me]
-    for load in loads:
-        load.wait()
-
-    def partial(offset, other):
-        rows = mixed_ref[:, seq.index(offset, other)].astype(jnp.float32)
-        rows = rows.reshape(blk_count * part_rows, depth).astype(jnp.bfloat16)
-        return [
-            lax.dot_general(
-                rows, gate_up[k], (((1,), (1,)), ((), ())), preferred_element_type=jnp.float32
-            )
-            for k in range(2)
-        ]
-
-    gate, up = reduce_over_seq(links, seq, partial, outgoing, from_sibling, from_pairs)
-    activation[seq.me] = (gate / (1.0 + jnp.exp(-gate)) * up).astype(jnp.bfloat16)
-    down_load.wait()
-    block_sum = BlockSum(links, grid, seq, parts, from_x, summed, from_z)
-
-    def use(s):
-        block_sum.put(
-            s, jnp.dot(activation[s], down[...], preferred_element_type=jnp.float32)
-        )
-
-    share_over_seq(links, seq, activation, use)
-    for s, total in block_sum.totals():
-        halves[s] = total.astype(jnp.bfloat16)
-    final_parts[seq.me] = halves[seq.me]
-    final_copies = [
-        links.send(halves.at[seq.index(*which)], final_parts.at[seq.me], seq.peer(*which))
-        for which in seq.everyone()
-    ]
-    for copy in mixed_copies + final_copies:
-        copy.wait_recv()
-    pieces = [final_parts[d].astype(jnp.float32) for d in range(seq_count)]
-    squares = sum(jnp.sum(piece * piece, axis=1, keepdims=True) for piece in pieces)
-    factor = lax.rsqrt(squares / (depth * seq_count) + EPSILON)
-    for d, piece in enumerate(pieces):
-        columns = slice(d * depth, (d + 1) * depth)
-        out_ref[:, columns] = (
-            mixed_parts[d].astype(jnp.float32) + piece * factor * gain_ref[:, columns]
-        ).astype(jnp.bfloat16)
-    links.finish()
-
-
-def feed(gate, up, down, mixed, gain, seq_count, blk_count):
-    units, depth = gate.shape
-    part_rows = mixed.shape[2]
-    row_count = part_rows * blk_count
-    pairs = seq_count // 2
-    bf16 = jnp.bfloat16
-    return pl.pallas_call(
-        functools.partial(feed_kernel, seq_count, blk_count),
-        out_shape=jax.ShapeDtypeStruct((part_rows, depth * seq_count), bf16),
-        in_specs=[ANY] * 3 + [VMEM] * 2,
-        out_specs=VMEM,
-        scratch_shapes=[
-            pltpu.VMEM((2, units, depth), bf16),
-            pltpu.VMEM((units, depth), bf16),
-            pltpu.VMEM((pairs, 2, 2, row_count, units), bf16),
-            pltpu.VMEM((pairs, 2, row_count, units), bf16),
-            pltpu.VMEM((pairs, 2, row_count, units), bf16),
-            pltpu.VMEM((seq_count, row_count, units), bf16),
-            pltpu.VMEM((seq_count, part_rows, depth), bf16),
-            pltpu.VMEM((seq_count, part_rows, depth), bf16),
-            pltpu.VMEM((seq_count, part_rows, depth), bf16),
-        ]
-        + block_sum_scratch(seq_count, blk_count, part_rows, depth)
-        + semaphores(5 * seq_count + seq_count * blk_count),
-        compiler_params=params(2),
-    )(gate, up, down, mixed, gain.reshape(1, -1))
+        gains[0].reshape(seq_count, 1, depth),
+        gains[1].reshape(1, -1),
+    )
 
 
 def attention_kernel(
@@ -850,17 +905,14 @@
         key_rows,
         value_rows,
     )
-    mixed = mix(
+    hidden_out = finish(
         weighted.reshape(seq_count, row_count, local_width),
         stats,
-        output_weight,
+        (output_weight, gate_weight.T, up_weight.T, down_weight),
         hidden,
-        attention_gain,
+        (attention_gain, feedforward_gain),
         seq_count,
         blk_count,
-    )
-    hidden_out = feed(
-        gate_weight.T, up_weight.T, down_weight, mixed, feedforward_gain, seq_count, blk_count
     )
     return (hidden_out, passage_keys[None], passage_values[None])
 

time: 173 us -> 161 us (0.931)
  Pallas kernels: 154 us -> 139 us
    pallas_call x2 -> x1, Pallas kernels: 105 us -> 88.3 us  [finish(): pl.pallas_call(functools.partial(finish_kernel, seq_count, blk_count), ou...]
    pallas_call x1, Pallas kernels: 36.2 us -> 38.5 us  [project(): pl.pallas_call(functools.partial(project_kernel, seq_count, blk_count), o...]
where the time goes in v3:
time: 161 us
  Pallas kernels  139 us (86%)
  local copies, waits for them, and re-layouts  12.3 us (8%)
  other arithmetic  6.8 us (4%)
  between operations  2.8 us (2%)
    pallas_call x1, Pallas kernels, finish(): pl.pallas_call(functools.partial(finish_kernel, seq_count, blk_count), ou...  88.3 us
    pallas_call x1, Pallas kernels, project(): pl.pallas_call(functools.partial(project_kernel, seq_count, blk_count), o...  38.5 us
    pallas_call x1, Pallas kernels, attend(): pl.pallas_call(attention_kernel, grid=(head_count, total_rows // block),...  12.1 us
    unnamed x23, local copies, waits for them, and re-layouts  7.07 us

profile of v3, /device:TPU:0, one launch (start us, length us, event | category | flops | bytes accessed | tf_op | source)
XLA Modules:
  0.0 160.7 jit_solution(2910111755917800787)
XLA Ops:
  0.7 1.4 dynamic_slice.29
  2.7 0.7 dynamic-slice_bitcast_fusion
  3.5 0.8 select_reduce_fusion.2
  4.8 0.6 dynamic_slice.28
  5.4 0.6 dynamic_slice.30
  6.6 0.8 select_reduce_fusion
  7.4 0.6 dynamic_slice.27
  8.7 0.6 dynamic_slice.26
  9.8 0.8 broadcast_add_fusion
  10.5 0.7 minimum_select_fusion
  11.3 1.3 subtract_select_fusion
  12.6 0.3 fusion
  12.9 0.7 pad_maximum_fusion.1.sine_ref
  13.6 0.7 pad_maximum_fusion.cosine_ref
  14.7 38.5 %shard_map.193 = (bf16[4,128,1024]{2,1,0:T(8,128)(2,1)}, bf16[4,128,512]{2,1,0:T(8,128)(2,1)}, f32[4,128,1]{2,1,0:T(8,128)}, bf16[128,512]{1,0:T(8,128)(2,1)}, bf16[128,512]{1,0:T(8,128)(2,1)}) custom-call(bf16[128,4096]{1,0:T(8,128)(2,1)} %states_ref.1, bf16[1024,512]{1,0:T(8,128)(2,1)} %query_weight.1, bf16[1024,512]{1,0:T(8,128)(2,1)} %key_weight.1, ...), custom_call_target="tpu_custom_call" | custom-call | tf_op jit(solution)/shard_map/pallas_call | solution.py:366
  53.2 1.2 copy-done.5
  54.4 0.9 copy-done.6
  55.4 0.9 copy-done.7
  56.3 0.9 copy-done.8
  57.2 12.1 %shard_map.194 = (bf16[1024,512]{1,0:T(8,128)(2,1)}, bf16[1024,512]{1,0:T(8,128)(2,1)}, bf16[512,512]{1,0:T(8,128)(2,1)S(1)}, f32[4,8,512]{2,1,0:T(8,128)S(1)}) custom-call(bf16[512,512]{1,0:T(8,128)(2,1)S(1)} %bitcast.34, f32[512,1]{1,0:T(8,128)S(1)} %bitcast.36, s32[512,1]{1,0:T(8,128)S(1)} %copy.27.old_limit_ref, s32[512,1]{1,0:T(8,128)S(1)} %copy.28.new_limit_ref, ...), custom_call_target="tpu_custom_call" | custom-call | tf_op jit(solution)/shard_map/pallas_call | solution.py:760
  69.3 1.2 copy-done.3
  70.5 1.2 copy-done.4
  71.8 88.3 %shard_map.195 = bf16[16,4096]{1,0:T(8,128)(2,1)S(1)} custom-call(bf16[4,128,512]{2,1,0:T(8,128)(2,1)S(1)} %bitcast.35, f32[4,8,512]{2,1,0:T(8,128)S(1)} %get-tuple-element.17.stats_ref, bf16[512,1024]{1,0:T(8,128)(2,1)S(1)} %copy-done.3, bf16[1376,1024]{1,0:T(8,128)(2,1)S(1)} %bitcast.30, bf16[1376,1024]{1,0:T(8,128)(2,1)} %bitcast.39, ...), custom_call_target="tpu_custom_call" | custom-call | tf_op jit(solution)/shard_map/pallas_call | solution.py:641
  160.1 0.7 copy.30
  (41 shorter events, 1.5 us)
Async XLA Ops:
  0.6 52.6 %copy-start.2 = (bf16[1,1024,512]{2,1,0:T(8,128)(2,1)S(1)}, bf16[1,1024,512]{2,1,0:T(8,128)(2,1)}, u32[]{:S(2)}) copy-start(bf16[1,1024,512]{2,1,0:T(8,128)(2,1)} %param.31) | copy-start | bytes 3145732
  0.6 52.6 %copy-start.1 = (bf16[1,1024,512]{2,1,0:T(8,128)(2,1)S(1)}, bf16[1,1024,512]{2,1,0:T(8,128)(2,1)}, u32[]{:S(2)}) copy-start(bf16[1,1024,512]{2,1,0:T(8,128)(2,1)} %param.30) | copy-start | bytes 3145732
  14.7 54.6 %copy-start.9 = (f32[4096]{0:T(1024)S(1)}, f32[4096]{0:T(1024)}, u32[]{:S(2)}) copy-start(f32[4096]{0:T(1024)} %param.25) | copy-start | bytes 49156
  14.7 54.6 %copy-start.10 = (f32[4096]{0:T(1024)S(1)}, f32[4096]{0:T(1024)}, u32[]{:S(2)}) copy-start(f32[4096]{0:T(1024)} %param.29) | copy-start | bytes 49156
  53.2 16.1 %copy-start = (bf16[1024,1376]{0,1:T(8,128)(2,1)S(1)}, bf16[1024,1376]{0,1:T(8,128)(2,1)}, u32[]{:S(2)}) copy-start(bf16[1024,1376]{0,1:T(8,128)(2,1)} %param.26) | copy-start | bytes 8454148
  53.2 1.2 copy-start.5
  54.4 0.9 copy-start.6
  55.4 0.9 copy-start.7
  56.3 0.9 copy-start.8
  69.3 1.2 copy-start.3
  70.5 1.2 copy-start.4

commit v4 on v3

--- a/solution.py
+++ b/solution.py
@@ -1,8 +1,8 @@
 import functools
-import math
 
 import jax
 import jax.numpy as jnp
+import numpy as np
 from jax import lax
 from jax.experimental import pallas as pl
 from jax.experimental.pallas import tpu as pltpu
@@ -20,6 +20,7 @@
 MESH = pl.DeviceIdType.MESH
 ANY = pl.BlockSpec(memory_space=pl.ANY)
 VMEM = pl.BlockSpec(memory_space=pltpu.VMEM)
+SMEM = pl.BlockSpec(memory_space=pltpu.SMEM)
 
 
 def greet(peers):
@@ -262,13 +263,20 @@
     value_weight,
     query_gain,
     key_gain,
-    cosine_ref,
-    sine_ref,
+    frequency_ref,
+    recompute_ref,
+    order_ref,
+    separators_ref,
+    lengths_ref,
     hidden_ref,
     queries_ref,
     factors_ref,
     key_rows_ref,
     value_rows_ref,
+    old_limit_ref,
+    new_limit_ref,
+    picked_ref,
+    turn_ref,
     outgoing,
     from_sibling,
     from_pairs,
@@ -276,6 +284,7 @@
     squares,
     landing,
     sums,
+    chosen,
     *sems,
 ):
     seq = Pairs(seq_count)
@@ -299,6 +308,23 @@
         arrivals[which] = links.send(
             states_ref.at[:, pl.ds(column, depth)], hidden_ref.at[seq.me], seq.peer(*which)
         )
+    chosen[:, :SEL] = recompute_ref[...]
+    lane = lax.broadcasted_iota(jnp.int32, (1, row_count), 1)
+    limits, my_positions, my_start, my_picked = layout(
+        seq.me, seq_count, order_ref, separators_ref, lengths_ref, chosen, lane
+    )
+    picked_ref[...] = jnp.where(lane < SEL, my_picked, -1)
+    limits = columns_of(jnp.concatenate(limits + [my_positions]).astype(jnp.float32))
+    for d in range(seq_count):
+        old_limit_ref[d] = limits[:, 2 * d : 2 * d + 1]
+        new_limit_ref[d] = limits[:, 2 * d + 1 : 2 * d + 2]
+    frequency = frequency_ref[...]
+    side = jnp.where(lane < HD // 2, -1.0, 1.0)
+    turn_angles = my_start.astype(jnp.float32) * frequency
+    turn_ref[0:1, :] = jnp.cos(turn_angles)
+    turn_ref[1:2, :] = jnp.sin(turn_angles) * side
+    angles = limits[:, 2 * seq_count : 2 * seq_count + 1] * frequency
+    cosine, sine = jnp.cos(angles), jnp.sin(angles) * side
     for load in loads:
         load.wait()
 
@@ -324,7 +350,7 @@
 
     def turned(raw, gain, h):
         piece = raw[:, h * HD : (h + 1) * HD] * gain[:, h * HD : (h + 1) * HD]
-        return piece * cosine_ref[...] + pltpu.roll(piece, HD // 2, 1) * sine_ref[...]
+        return piece * cosine + pltpu.roll(piece, HD // 2, 1) * sine
 
     for h in range(width // HD):
         queries_ref[seq.me, :, h * HD : (h + 1) * HD] = turned(query, query_gain, h).astype(
@@ -358,7 +384,9 @@
     links.finish()
 
 
-def project(states, weights, gains, cosine, sine, seq_count, blk_count):
+def project(
+    states, weights, gains, recompute_index, passage_order, separators, lengths, seq_count, blk_count
+):
     row_count = states.shape[0]
     depth, width = weights[0].shape
     pairs = seq_count // 2
@@ -371,9 +399,13 @@
             jax.ShapeDtypeStruct((seq_count, row_count, 1), f32),
             jax.ShapeDtypeStruct((row_count, width), bf16),
             jax.ShapeDtypeStruct((row_count, width), bf16),
+            jax.ShapeDtypeStruct((seq_count, row_count, 1), f32),
+            jax.ShapeDtypeStruct((seq_count, row_count, 1), f32),
+            jax.ShapeDtypeStruct((1, row_count), jnp.int32),
+            jax.ShapeDtypeStruct((8, HD), f32),
         ],
-        in_specs=[ANY] * 4 + [VMEM] * 4,
-        out_specs=[VMEM] * 5,
+        in_specs=[ANY] * 4 + [VMEM] * 4 + [SMEM] * 3,
+        out_specs=[VMEM] * 9,
         scratch_shapes=[
             pltpu.VMEM((pairs, 2, 3, row_count, width), bf16),
             pltpu.VMEM((pairs, 3, row_count, width), bf16),
@@ -382,10 +414,20 @@
             pltpu.VMEM((8, row_count), f32),
             pltpu.VMEM((blk_count, 8, row_count), f32),
             pltpu.VMEM((seq_count, 8, row_count), f32),
+            pltpu.VMEM((seq_count, row_count), jnp.int32),
         ]
         + semaphores(5 * seq_count + blk_count),
         compiler_params=params(0, 60),
-    )(states, *weights, *[g.reshape(1, width) for g in gains], cosine, sine)
+    )(
+        states,
+        *weights,
+        *[g.reshape(1, width) for g in gains],
+        frequencies(),
+        recompute_index,
+        passage_order,
+        separators,
+        lengths,
+    )
 
 
 def finish_kernel(
@@ -407,6 +449,7 @@
     weight,
     squares,
     landing,
+    hidden,
     parts,
     from_x,
     summed,
@@ -434,6 +477,7 @@
     load = links.move(weight_ref, weight)
     gate_loads = [links.move(gate_ref, gate_up.at[0]), links.move(up_ref, gate_up.at[1])]
     down_load = links.move(down_ref, down)
+    hidden_load = links.move(hidden_ref.at[:, grid.me], hidden)
 
     def stats_for(index):
         return stats_ref.at[:, :, pl.ds(pl.multiple_of(index * row_count, row_count), row_count)]
@@ -453,6 +497,7 @@
     for copy in copies:
         copy.wait_recv()
     load.wait()
+    hidden_load.wait()
     head_count = width // HD
     shares = []
     for h in range(head_count):
@@ -491,9 +536,7 @@
         copy.wait_recv()
     factor = lax.rsqrt(jnp.sum(squares[...], axis=0) / (depth * seq_count) + EPSILON)
     update = landing[...] * factor[:, :, 0:1] * attention_gain[seq.me]
-    mixed[grid.z, grid.x] = (hidden_ref[:, grid.me].astype(jnp.float32) + update).astype(
-        jnp.bfloat16
-    )
+    mixed[grid.z, grid.x] = (hidden[...].astype(jnp.float32) + update).astype(jnp.bfloat16)
 
     chunks = grid.depth
     order = list(range(1, seq.pairs)) + [0]
@@ -562,11 +605,13 @@
             act_far[c, offset] = links.send(block, block, seq.peer(offset, 0))
         act_near[c] = [links.send(block, block, seq.peer(0, 1))]
 
-    def multiply_down(c):
+    def pass_activation(c):
         for offset in order[:-1]:
             act_far[c, seq.pairs - offset].wait_recv()
             block = activation.at[c, seq.index(offset, 0)]
             act_near[c].append(links.send(block, block, seq.peer(0, 1)))
+
+    def multiply_down(c):
         for copy in act_near[c]:
             copy.wait_recv()
         rows = activation[c].astype(jnp.float32)
@@ -599,13 +644,16 @@
             multiply_gate_up(step)
             if step + 1 < chunks:
                 pass_mixed(step + 1)
+        if 0 <= step - 2 < chunks:
+            pass_activation(step - 2)
+        if 0 <= step - 3 < chunks:
+            sum_over_x(step - 3)
+        if step < chunks:
             send_pair_sums(step)
         if 0 <= step - 1 < chunks:
             activate(step - 1)
         if 0 <= step - 2 < chunks:
             multiply_down(step - 2)
-        if 0 <= step - 3 < chunks:
-            sum_over_x(step - 3)
     total = feed_summed[0].astype(jnp.float32)
     for c in range(1, chunks):
         sum_copies[c].wait_recv()
@@ -641,7 +689,7 @@
     return pl.pallas_call(
         functools.partial(finish_kernel, seq_count, blk_count),
         out_shape=jax.ShapeDtypeStruct((part_rows, depth * seq_count), bf16),
-        in_specs=[ANY] * 6 + [VMEM] * 3,
+        in_specs=[ANY] * 7 + [VMEM] * 2,
         out_specs=VMEM,
         scratch_shapes=[
             pltpu.VMEM((seq_count, row_count, width), bf16),
@@ -650,6 +698,7 @@
             pltpu.VMEM((width, depth), bf16),
             pltpu.VMEM((seq_count, seq_count, part_rows, HD), f32),
             pltpu.VMEM((seq_count, part_rows, depth), f32),
+            pltpu.VMEM((seq_count, part_rows, depth), bf16),
         ]
         + block_sum_scratch(seq_count, blk_count, part_rows, depth)
         + [
@@ -669,7 +718,7 @@
             pltpu.VMEM((chunks, seq_count, part_rows, depth), bf16),
         ]
         + semaphores(8 * seq_count + (2 * seq_count + 3) * blk_count),
-        compiler_params=params(1, 48),
+        compiler_params=params(1, 60),
     )(
         weighted,
         stats,
@@ -713,7 +762,8 @@
             replaced, new_values, old_values_ref[...].astype(jnp.float32)
         ).astype(jnp.bfloat16)
 
-    query = (query_ref[...].astype(jnp.float32) * factor_ref[...]).astype(jnp.bfloat16)
+    factor = factor_ref[...] * HD ** (-0.5)
+    query = (query_ref[...].astype(jnp.float32) * factor).astype(jnp.bfloat16)
     contract = (((1,), (1,)), ((), ()))
     old_scores = lax.dot_general(
         query, keys_ref[...], contract, preferred_element_type=jnp.float32
@@ -721,17 +771,18 @@
     new_scores = lax.dot_general(
         query, key_rows_ref[...], contract, preferred_element_type=jnp.float32
     )
-    scale = HD ** (-0.5)
-    old_seen = lax.broadcasted_iota(jnp.int32, old_scores.shape, 1) <= old_limit_ref[...]
+    old_seen = lax.broadcasted_iota(jnp.int32, old_scores.shape, 1) <= old_limit_ref[...].astype(
+        jnp.int32
+    )
     new_token = lax.broadcasted_iota(jnp.int32, new_scores.shape, 1) - SEL
-    new_seen = (new_token >= 0) & (new_token <= new_limit_ref[...])
-    old_scores = jnp.where(old_seen, old_scores * scale, MASKED_SCORE)
-    new_scores = jnp.where(new_seen, new_scores * scale, MASKED_SCORE)
+    new_seen = (new_token >= 0) & (new_token <= new_limit_ref[...].astype(jnp.int32))
+    old_scores = jnp.where(old_seen, old_scores, MASKED_SCORE)
+    new_scores = jnp.where(new_seen, new_scores, MASKED_SCORE)
     peak = jnp.maximum(
         jnp.max(old_scores, axis=1, keepdims=True), jnp.max(new_scores, axis=1, keepdims=True)
     )
-    old_weights = jnp.where(old_seen, jnp.exp(old_scores - peak), 0.0)
-    new_weights = jnp.where(new_seen, jnp.exp(new_scores - peak), 0.0)
+    old_weights = jnp.exp(old_scores - peak)
+    new_weights = jnp.exp(new_scores - peak)
     total = jnp.sum(old_weights, axis=1, keepdims=True) + jnp.sum(
         new_weights, axis=1, keepdims=True
     )
@@ -784,7 +835,7 @@
             tile,
             pl.BlockSpec((1, 8, block), lambda h, i: (h, 0, i)),
         ],
-        compiler_params=pltpu.CompilerParams(vmem_limit_bytes=48 * 1024 * 1024),
+        compiler_params=pltpu.CompilerParams(vmem_limit_bytes=60 * 1024 * 1024),
     )(
         queries,
         factor,
@@ -800,33 +851,50 @@
 
 
 def frequencies():
-    indices = jnp.arange(HD // 2, dtype=jnp.float32)
-    return jnp.exp(indices * (-2.0 * math.log(ROPE_THETA) / HD))
-
-
-def layout(passage_order, separators, recompute_index, seq_count):
-    devices = jnp.arange(seq_count, dtype=jnp.int32)
-    slots = jnp.arange(PPR, dtype=jnp.int32)
-    earlier = slots[None, :, None] >= slots[None, None, :]
-    opening = slots[None, :] * PLEN + jnp.sum(
-        jnp.where(earlier, separators[:, None, :], 0), axis=2
-    )
-    hit = passage_order[None, :] == devices[:, None]
-    starts = jnp.sum(jnp.where(hit, opening.reshape(-1)[None, :], 0), axis=1)
-    owners = jnp.sum(jnp.where(hit, (devices // PPR)[None, :], 0), axis=1)
-    prompt_start = jnp.repeat(opening[:, PPR - 1] + PLEN, PPR)
-    offsets = (devices % PPR) * TOKN_DEV
-    new_starts = prompt_start + offsets
-    new_positions = new_starts[:, None] + jnp.arange(TOKN_DEV, dtype=jnp.int32)[None, :]
-    positions = jnp.concatenate([starts[:, None] + recompute_index, new_positions], axis=1)
-    requests = jnp.concatenate(
-        [
-            jnp.broadcast_to(owners[:, None], recompute_index.shape),
-            jnp.broadcast_to((devices // PPR)[:, None], new_positions.shape),
-        ],
-        axis=1,
-    )
-    return starts, owners, new_starts, offsets, positions, requests
+    exponents = np.arange(HD // 2, dtype=np.float64) * (-2.0 / HD)
+    return np.tile((ROPE_THETA**exponents).astype(np.float32), 2).reshape(1, HD)
+
+
+def layout(me, seq_count, order, separators, lengths, chosen, lane):
+    requests = seq_count // PPR
+    openings = []
+    for r in range(requests):
+        passed = 0
+        for slot in range(PPR):
+            passed = passed + separators[r, slot]
+            openings.append(passed + slot * PLEN)
+
+    def select(pairs):
+        return sum(jnp.where(hit, value, 0) for hit, value in pairs)
+
+    starts, owners, new_starts = [], [], []
+    for d in range(seq_count):
+        hits = [order[k] == d for k in range(seq_count)]
+        starts.append(select(zip(hits, openings)))
+        owners.append(select((hit, k // PPR) for k, hit in enumerate(hits)))
+        base = openings[(d // PPR) * PPR + PPR - 1] + PLEN
+        new_starts.append(base + (d % PPR) * TOKN_DEV)
+    here = [me == d for d in range(seq_count)]
+    my_start = select(zip(here, starts))
+    my_owner = select(zip(here, owners))
+    my_new_start = select(zip(here, new_starts))
+    my_request = lax.div(me, PPR)
+    my_length = select((my_request == r, lengths[r]) for r in range(requests))
+    last_live = my_length - 1 - lax.rem(me, PPR) * TOKN_DEV
+    rows, my_positions, my_picked = [], 0, 0
+    for d in range(seq_count):
+        picked = chosen[d : d + 1, :]
+        positions = jnp.where(lane < SEL, starts[d] + picked, new_starts[d] + lane - SEL)
+        request = jnp.where(lane < SEL, owners[d], d // PPR)
+        rows.append(jnp.where(request == my_owner, positions - my_start, -1))
+        rows.append(
+            jnp.where(
+                request == my_request, jnp.minimum(positions - my_new_start, last_live), -1
+            )
+        )
+        my_positions = my_positions + jnp.where(here[d], positions, 0)
+        my_picked = my_picked + jnp.where(here[d], picked, 0)
+    return rows, my_positions, my_start, my_picked
 
 
 def shards(
@@ -851,45 +919,18 @@
 ):
     seq_count = lax.axis_size("seq")
     blk_count = lax.axis_size("blk")
-    seq_index = lax.axis_index("seq")
     row_count = hidden_states.shape[0]
     local_width = query_weight.shape[1]
     total_rows = row_count * seq_count
 
-    def mine(array):
-        return lax.dynamic_index_in_dim(array, seq_index, 0, keepdims=False)
-
-    starts, owners, new_starts, offsets, positions, requests = layout(
-        passage_order, separators, recompute_index, seq_count
-    )
-    frequency = frequencies()
-    passage_start = mine(starts)
-    own_request = seq_index // PPR
-    old_limit = jnp.where(requests == mine(owners), positions - passage_start, -1)
-    live_limit = lax.dynamic_index_in_dim(prompt_lengths, own_request, 0, False) - 1 - mine(offsets)
-    new_limit = jnp.where(
-        requests == own_request, jnp.minimum(positions - mine(new_starts), live_limit), -1
-    )
-    picked = jnp.concatenate(
-        [mine(recompute_index), jnp.full((row_count - SEL,), -1, jnp.int32)]
-    ).reshape(1, row_count)
-    turn_angles = passage_start.astype(jnp.float32) * frequency
-    turn_cosine, turn_sine = jnp.cos(turn_angles), jnp.sin(turn_angles)
-    turn = jnp.concatenate(
-        [
-            jnp.concatenate([turn_cosine, turn_cosine])[None],
-            jnp.concatenate([-turn_sine, turn_sine])[None],
-            jnp.zeros((6, HD), jnp.float32),
-        ]
-    )
-    angles = mine(positions).astype(jnp.float32)[:, None] * frequency[None, :]
-    cosine, sine = jnp.cos(angles), jnp.sin(angles)
-    hidden, queries, factors, key_rows, value_rows = project(
+    hidden, queries, factors, key_rows, value_rows, old_limit, new_limit, picked, turn = project(
         hidden_states,
         (query_weight, key_weight, value_weight),
         (query_gain, key_gain),
-        jnp.concatenate([cosine, cosine], axis=1),
-        jnp.concatenate([-sine, sine], axis=1),
+        recompute_index,
+        passage_order,
+        separators,
+        prompt_lengths,
         seq_count,
         blk_count,
     )

time: 161 us -> 147 us (0.913)
  local copies, waits for them, and re-layouts: 12.3 us -> 1.57 us
  other arithmetic: 6.8 us -> 0 us
  Pallas kernels: 139 us -> 145 us
  between operations: 2.8 us -> 0.65 us
    pallas_call x1, Pallas kernels: 88.3 us -> 94 us  [finish(): pl.pallas_call(functools.partial(finish_kernel, seq_count, blk_count), ou...]
    unnamed x23 -> x1, local copies, waits for them, and re-layouts: 7.07 us -> 1.57 us
    dynamic_slice x5 -> x0, local copies, waits for them, and re-layouts: 3.74 us -> none  [the longest x4 2.36 us: mine(): return lax.dynamic_index_in_dim(array, seq_index, 0, keepdims=False)]
    select_n x3 -> x0, other arithmetic: 2 us -> none  [the longest x1 1.28 us: shards(): jnp.where(requests == mine(owners), positions - passage_start, -1)]
    reduce_sum x2 -> x0, other arithmetic: 1.62 us -> none  [the longest x1 0.82 us: layout(): jnp.sum(jnp.where(earlier, separators[:, None, :], 0), axis=2)]
where the time goes in v4:
time: 147 us
  Pallas kernels  145 us (99%)
  local copies, waits for them, and re-layouts  1.57 us (1%)
    pallas_call x1, Pallas kernels, finish(): pl.pallas_call(functools.partial(finish_kernel, seq_count, blk_count), ou...  94 us
    pallas_call x1, Pallas kernels, project(): pl.pallas_call(functools.partial(project_kernel, seq_count, blk_count), o...  38.6 us
    pallas_call x1, Pallas kernels, attend(): pl.pallas_call(attention_kernel, grid=(head_count, total_rows // block),...  12.3 us

profile of v4, /device:TPU:0, one launch (start us, length us, event | category | flops | bytes accessed | tf_op | source)
XLA Modules:
  0.0 147.1 jit_solution(13369732494704826314)
XLA Ops:
  0.6 38.6 %shard_map.202 = (bf16[4,128,1024]{2,1,0:T(8,128)(2,1)}, bf16[4,128,512]{2,1,0:T(8,128)(2,1)}, f32[4,128,1]{2,1,0:T(8,128)}, bf16[128,512]{1,0:T(8,128)(2,1)}, b...) custom-call(bf16[128,4096]{1,0:T(8,128)(2,1)} %states_ref.1, ...), custom_call_target="tpu_custom_call" | custom-call | tf_op jit(solution)/shard_map/pallas_call | solution.py:394
  39.3 12.3 %shard_map.203 = (bf16[1024,512]{1,0:T(8,128)(2,1)}, bf16[1024,512]{1,0:T(8,128)(2,1)}, bf16[512,512]{1,0:T(8,128)(2,1)}, f32[4,8,512]{2,1,0:T(8,128)}) custom-call(bf16[512,512]{1,0:T(8,128)(2,1)} %bitcast.21, f32[512,1]{1,0:T(8,128)} %bitcast.23, f32[512,1]{1,0:T(8,128)} %bitcast.24, f32[512,1]{1,0:T(8,128)} %bitcast.25, ...), custom_call_target="tpu_custom_call" | custom-call | tf_op jit(solution)/shard_map/pallas_call | solution.py:811
  51.6 94.0 %shard_map.204 = bf16[16,4096]{1,0:T(8,128)(2,1)} custom-call(bf16[4,128,512]{2,1,0:T(8,128)(2,1)} %bitcast.22, f32[4,8,512]{2,1,0:T(8,128)} %get-tuple-element.25.stats_ref, bf16[512,1024]{1,0:T(8,128)(2,1)} %weight_ref.1, bf16[1376,1024]{1,0:T(8,128)(2,1)} %bitcast.16, bf16[1376,1024]{1,0:T(8,128)(2,1)} %bitcast.17, bf16[1376,1024]{1,0:T(8,128)(2,1)} %down_ref.1, ...), custom_call_target="tpu_custom_call" | custom-call | tf_op jit(solution)/shard_map/pallas_call | solution.py:689
  145.6 1.6 %copy.23 = bf16[16,4096]{1,0:T(8,128)(2,1)} copy(bf16[16,4096]{1,0:T(8,128)(2,1)} %shard_map.204) | data formatting | bytes 262144

commit v5 on v4

--- a/solution.py
+++ b/solution.py
@@ -430,19 +430,85 @@
     )
 
 
+def blend(h, picked, turn, old_keys, old_values, key_rows, value_rows, keys, values):
+    columns = slice(h * HD, (h + 1) * HD)
+    row_count = key_rows.shape[0]
+    token = lax.broadcasted_iota(jnp.int32, (PLEN, row_count), 0)
+    chosen = jnp.where(token == picked, 1.0, 0.0)
+    replaced = jnp.max(chosen, axis=1, keepdims=True) > 0.5
+    chosen = chosen.astype(jnp.bfloat16)
+    old = old_keys[0, :, columns].astype(jnp.float32)
+    turned = old * turn[0:1, :] + pltpu.roll(old, HD // 2, 1) * turn[1:2, :]
+    new_keys = jnp.dot(chosen, key_rows[:, columns], preferred_element_type=jnp.float32)
+    keys[0, :, columns] = jnp.where(replaced, new_keys, turned).astype(jnp.bfloat16)
+    new_values = jnp.dot(chosen, value_rows[:, columns], preferred_element_type=jnp.float32)
+    values[0, :, columns] = jnp.where(
+        replaced, new_values, old_values[0, :, columns].astype(jnp.float32)
+    ).astype(jnp.bfloat16)
+
+
+def attend(h, query, old_limit, new_limit, keys, values, key_rows, value_rows):
+    columns = slice(h * HD, (h + 1) * HD)
+    contract = (((1,), (1,)), ((), ()))
+    old_scores = lax.dot_general(
+        query, keys[0, :, columns], contract, preferred_element_type=jnp.float32
+    )
+    new_scores = lax.dot_general(
+        query, key_rows[:, columns], contract, preferred_element_type=jnp.float32
+    )
+    old_seen = lax.broadcasted_iota(jnp.int32, old_scores.shape, 1) <= old_limit
+    new_token = lax.broadcasted_iota(jnp.int32, new_scores.shape, 1) - SEL
+    new_seen = (new_token >= 0) & (new_token <= new_limit)
+    old_scores = jnp.where(old_seen, old_scores, MASKED_SCORE)
+    new_scores = jnp.where(new_seen, new_scores, MASKED_SCORE)
+    peak = jnp.maximum(
+        jnp.max(old_scores, axis=1, keepdims=True), jnp.max(new_scores, axis=1, keepdims=True)
+    )
+    old_weights = jnp.exp(old_scores - peak)
+    new_weights = jnp.exp(new_scores - peak)
+    total = jnp.sum(old_weights, axis=1, keepdims=True) + jnp.sum(
+        new_weights, axis=1, keepdims=True
+    )
+    weighted = jnp.dot(
+        old_weights.astype(jnp.bfloat16),
+        values[0, :, columns],
+        preferred_element_type=jnp.float32,
+    ) + jnp.dot(
+        new_weights.astype(jnp.bfloat16),
+        value_rows[:, columns],
+        preferred_element_type=jnp.float32,
+    )
+    lane = lax.broadcasted_iota(jnp.int32, weighted.shape, 1)
+    return weighted.astype(jnp.bfloat16), jnp.transpose(jnp.where(lane == 0, peak, total))[:8]
+
+
 def finish_kernel(
     seq_count,
     blk_count,
-    weighted_ref,
-    stats_ref,
     weight_ref,
     gate_ref,
     up_ref,
     down_ref,
     hidden_ref,
+    old_keys_ref,
+    old_values_ref,
+    queries_ref,
+    factors_ref,
+    old_limit_ref,
+    new_limit_ref,
+    picked_ref,
+    turn_ref,
+    key_rows_ref,
+    value_rows_ref,
     attention_gain,
     feed_gain,
     out_ref,
+    keys_ref,
+    values_ref,
+    old_keys,
+    old_values,
+    weighted,
+    own_stats,
     partials,
     stats,
     attention,
@@ -474,47 +540,72 @@
     row_count, width = attention.shape[1:]
     part_rows, depth = mixed.shape[3:]
     links = Links(*sems)
+    cache_loads = [links.move(old_keys_ref, old_keys), links.move(old_values_ref, old_values)]
     load = links.move(weight_ref, weight)
     gate_loads = [links.move(gate_ref, gate_up.at[0]), links.move(up_ref, gate_up.at[1])]
     down_load = links.move(down_ref, down)
     hidden_load = links.move(hidden_ref.at[:, grid.me], hidden)
-
-    def stats_for(index):
-        return stats_ref.at[:, :, pl.ds(pl.multiple_of(index * row_count, row_count), row_count)]
-
-    own = [
-        links.move(weighted_ref.at[seq.me], partials.at[seq.me]),
-        links.move(stats_for(seq.me), stats.at[seq.me]),
-    ]
     greet([seq.peer(*which) for which in seq.everyone()] + grid.neighbours())
+    for cache_load in cache_loads:
+        cache_load.wait()
+    head_count = width // HD
+    group = min(seq_count, 4)
     copies = []
-    for which in seq.everyone():
-        index = seq.index(*which)
-        copies.append(links.send(stats_for(index), stats.at[seq.me], seq.peer(*which)))
-        copies.append(links.send(weighted_ref.at[index], partials.at[seq.me], seq.peer(*which)))
-    for copy in own:
-        copy.wait()
+    for h in range(head_count):
+        columns = slice(h * HD, (h + 1) * HD)
+        blend(
+            h,
+            picked_ref[...],
+            turn_ref,
+            old_keys,
+            old_values,
+            key_rows_ref,
+            value_rows_ref,
+            keys_ref,
+            values_ref,
+        )
+        for first in range(0, seq_count, group):
+            some = slice(first, first + group)
+            rows = group * row_count
+            factor = factors_ref[some].reshape(rows, 1) * HD ** (-0.5)
+            query = queries_ref[some, :, columns].reshape(rows, HD).astype(jnp.float32) * factor
+            values, tile = attend(
+                h,
+                query.astype(jnp.bfloat16),
+                old_limit_ref[some].reshape(rows, 1).astype(jnp.int32),
+                new_limit_ref[some].reshape(rows, 1).astype(jnp.int32),
+                keys_ref,
+                values_ref,
+                key_rows_ref,
+                value_rows_ref,
+            )
+            for d in range(group):
+                at = slice(d * row_count, (d + 1) * row_count)
+                weighted[h, first + d] = values[at]
+                own_stats[h, first + d] = tile[:, at]
+        for which in seq.everyone():
+            index, peer = seq.index(*which), seq.peer(*which)
+            copies.append(links.send(own_stats.at[h, index], stats.at[h, seq.me], peer))
+            copies.append(links.send(weighted.at[h, index], partials.at[h, seq.me], peer))
+        stats[h, seq.me] = own_stats[h, seq.me]
+        partials[h, seq.me] = weighted[h, seq.me]
     for copy in copies:
         copy.wait_recv()
     load.wait()
     hidden_load.wait()
-    head_count = width // HD
     shares = []
     for h in range(head_count):
-        peaks = [stats[d, h, 0:1, :] for d in range(seq_count)]
+        peaks = [stats[h, d, 0:1, :] for d in range(seq_count)]
         top = functools.reduce(jnp.maximum, peaks)
         scales = [jnp.exp(peak - top) for peak in peaks]
-        total = sum(scale * stats[d, h, 1:2, :] for d, scale in enumerate(scales))
+        total = sum(scale * stats[h, d, 1:2, :] for d, scale in enumerate(scales))
         shares += [scale / total for scale in scales]
     shares = columns_of(jnp.concatenate(shares))
     for h in range(head_count):
         merged = jnp.zeros((row_count, HD), jnp.float32)
         for d in range(seq_count):
             column = h * seq_count + d
-            merged += (
-                partials[d, :, h * HD : (h + 1) * HD].astype(jnp.float32)
-                * shares[:, column : column + 1]
-            )
+            merged += partials[h, d].astype(jnp.float32) * shares[:, column : column + 1]
         attention[seq.me, :, h * HD : (h + 1) * HD] = merged.astype(jnp.bfloat16)
     block_sum = BlockSum(links, grid, seq, parts, from_x, summed, from_z)
 
@@ -677,8 +768,8 @@
     links.finish()
 
 
-def finish(weighted, stats, weights, hidden, gains, seq_count, blk_count):
-    row_count = weighted.shape[1]
+def finish(weights, hidden, caches, rows, gains, seq_count, blk_count):
+    row_count = hidden.shape[1]
     width, depth = weights[0].shape
     units = weights[1].shape[0]
     part_rows = row_count // blk_count
@@ -688,12 +779,20 @@
     bf16, f32 = jnp.bfloat16, jnp.float32
     return pl.pallas_call(
         functools.partial(finish_kernel, seq_count, blk_count),
-        out_shape=jax.ShapeDtypeStruct((part_rows, depth * seq_count), bf16),
-        in_specs=[ANY] * 7 + [VMEM] * 2,
-        out_specs=VMEM,
+        out_shape=[
+            jax.ShapeDtypeStruct((part_rows, depth * seq_count), bf16),
+            jax.ShapeDtypeStruct(caches[0].shape, bf16),
+            jax.ShapeDtypeStruct(caches[1].shape, bf16),
+        ],
+        in_specs=[ANY] * 7 + [VMEM] * 10,
+        out_specs=[VMEM] * 3,
         scratch_shapes=[
-            pltpu.VMEM((seq_count, row_count, width), bf16),
-            pltpu.VMEM((seq_count, width // HD, 8, row_count), f32),
+            pltpu.VMEM(caches[0].shape, bf16),
+            pltpu.VMEM(caches[1].shape, bf16),
+            pltpu.VMEM((width // HD, seq_count, row_count, HD), bf16),
+            pltpu.VMEM((width // HD, seq_count, 8, row_count), f32),
+            pltpu.VMEM((width // HD, seq_count, row_count, HD), bf16),
+            pltpu.VMEM((width // HD, seq_count, 8, row_count), f32),
             pltpu.VMEM((seq_count, row_count, width), bf16),
             pltpu.VMEM((width, depth), bf16),
             pltpu.VMEM((seq_count, seq_count, part_rows, HD), f32),
@@ -717,136 +816,15 @@
             pltpu.VMEM((chunks, seq_count, part_rows, depth), bf16),
             pltpu.VMEM((chunks, seq_count, part_rows, depth), bf16),
         ]
-        + semaphores(8 * seq_count + (2 * seq_count + 3) * blk_count),
+        + semaphores((8 + 2 * width // HD) * seq_count + (2 * seq_count + 3) * blk_count),
         compiler_params=params(1, 60),
     )(
-        weighted,
-        stats,
         *weights,
         hidden.reshape(seq_count, blk_count, part_rows, depth),
+        *caches,
+        *rows,
         gains[0].reshape(seq_count, 1, depth),
         gains[1].reshape(1, -1),
-    )
-
-
-def attention_kernel(
-    query_ref,
-    factor_ref,
-    old_limit_ref,
-    new_limit_ref,
-    picked_ref,
-    turn_ref,
-    old_keys_ref,
-    old_values_ref,
-    key_rows_ref,
-    value_rows_ref,
-    keys_ref,
-    values_ref,
-    weighted_ref,
-    stats_ref,
-):
-    @pl.when(pl.program_id(1) == 0)
-    def blend():
-        row_count = key_rows_ref.shape[0]
-        token = lax.broadcasted_iota(jnp.int32, (PLEN, row_count), 0)
-        hit = token == picked_ref[...]
-        chosen = jnp.where(hit, 1.0, 0.0)
-        replaced = jnp.max(chosen, axis=1, keepdims=True) > 0.5
-        chosen = chosen.astype(jnp.bfloat16)
-        old = old_keys_ref[...].astype(jnp.float32)
-        turned = old * turn_ref[0:1, :] + pltpu.roll(old, HD // 2, 1) * turn_ref[1:2, :]
-        new_keys = jnp.dot(chosen, key_rows_ref[...], preferred_element_type=jnp.float32)
-        keys_ref[...] = jnp.where(replaced, new_keys, turned).astype(jnp.bfloat16)
-        new_values = jnp.dot(chosen, value_rows_ref[...], preferred_element_type=jnp.float32)
-        values_ref[...] = jnp.where(
-            replaced, new_values, old_values_ref[...].astype(jnp.float32)
-        ).astype(jnp.bfloat16)
-
-    factor = factor_ref[...] * HD ** (-0.5)
-    query = (query_ref[...].astype(jnp.float32) * factor).astype(jnp.bfloat16)
-    contract = (((1,), (1,)), ((), ()))
-    old_scores = lax.dot_general(
-        query, keys_ref[...], contract, preferred_element_type=jnp.float32
-    )
-    new_scores = lax.dot_general(
-        query, key_rows_ref[...], contract, preferred_element_type=jnp.float32
-    )
-    old_seen = lax.broadcasted_iota(jnp.int32, old_scores.shape, 1) <= old_limit_ref[...].astype(
-        jnp.int32
-    )
-    new_token = lax.broadcasted_iota(jnp.int32, new_scores.shape, 1) - SEL
-    new_seen = (new_token >= 0) & (new_token <= new_limit_ref[...].astype(jnp.int32))
-    old_scores = jnp.where(old_seen, old_scores, MASKED_SCORE)
-    new_scores = jnp.where(new_seen, new_scores, MASKED_SCORE)
-    peak = jnp.maximum(
-        jnp.max(old_scores, axis=1, keepdims=True), jnp.max(new_scores, axis=1, keepdims=True)
-    )
-    old_weights = jnp.exp(old_scores - peak)
-    new_weights = jnp.exp(new_scores - peak)
-    total = jnp.sum(old_weights, axis=1, keepdims=True) + jnp.sum(
-        new_weights, axis=1, keepdims=True
-    )
-    weighted = jnp.dot(
-        old_weights.astype(jnp.bfloat16), values_ref[...], preferred_element_type=jnp.float32
-    ) + jnp.dot(
-        new_weights.astype(jnp.bfloat16), value_rows_ref[...], preferred_element_type=jnp.float32
-    )
-    weighted_ref[...] = weighted.astype(jnp.bfloat16)
-    lane = lax.broadcasted_iota(jnp.int32, weighted.shape, 1)
-    stats = jnp.transpose(jnp.where(lane == 0, peak, total))
-    stats_ref[0] = stats[:8, :]
-
-
-def attend(
-    queries, factor, old_limit, new_limit, picked, turn, old_keys, old_values, key_rows, value_rows
-):
-    total_rows, width = queries.shape
-    row_count = key_rows.shape[0]
-    head_count = width // HD
-    block = min(total_rows, 512)
-    by_row = pl.BlockSpec((block, 1), lambda h, i: (i, 0))
-    by_head = pl.BlockSpec((PLEN, HD), lambda h, i: (0, h))
-    rows_by_head = pl.BlockSpec((row_count, HD), lambda h, i: (0, h))
-    tile = pl.BlockSpec((block, HD), lambda h, i: (i, h))
-    return pl.pallas_call(
-        attention_kernel,
-        grid=(head_count, total_rows // block),
-        out_shape=[
-            jax.ShapeDtypeStruct((PLEN, width), jnp.bfloat16),
-            jax.ShapeDtypeStruct((PLEN, width), jnp.bfloat16),
-            jax.ShapeDtypeStruct((total_rows, width), jnp.bfloat16),
-            jax.ShapeDtypeStruct((head_count, 8, total_rows), jnp.float32),
-        ],
-        in_specs=[
-            tile,
-            by_row,
-            by_row,
-            by_row,
-            pl.BlockSpec((1, row_count), lambda h, i: (0, 0)),
-            pl.BlockSpec((8, HD), lambda h, i: (0, 0)),
-            by_head,
-            by_head,
-            rows_by_head,
-            rows_by_head,
-        ],
-        out_specs=[
-            by_head,
-            by_head,
-            tile,
-            pl.BlockSpec((1, 8, block), lambda h, i: (h, 0, i)),
-        ],
-        compiler_params=pltpu.CompilerParams(vmem_limit_bytes=60 * 1024 * 1024),
-    )(
-        queries,
-        factor,
-        old_limit,
-        new_limit,
-        picked,
-        turn,
-        old_keys,
-        old_values,
-        key_rows,
-        value_rows,
     )
 
 
@@ -919,10 +897,6 @@
 ):
     seq_count = lax.axis_size("seq")
     blk_count = lax.axis_size("blk")
-    row_count = hidden_states.shape[0]
-    local_width = query_weight.shape[1]
-    total_rows = row_count * seq_count
-
     hidden, queries, factors, key_rows, value_rows, old_limit, new_limit, picked, turn = project(
         hidden_states,
         (query_weight, key_weight, value_weight),
@@ -934,28 +908,15 @@
         seq_count,
         blk_count,
     )
-    passage_keys, passage_values, weighted, stats = attend(
-        queries.reshape(total_rows, local_width),
-        factors.reshape(total_rows, 1),
-        old_limit.reshape(total_rows, 1),
-        new_limit.reshape(total_rows, 1),
-        picked,
-        turn,
-        cached_keys[0],
-        cached_values[0],
-        key_rows,
-        value_rows,
-    )
-    hidden_out = finish(
-        weighted.reshape(seq_count, row_count, local_width),
-        stats,
+    return finish(
         (output_weight, gate_weight.T, up_weight.T, down_weight),
         hidden,
+        (cached_keys, cached_values),
+        (queries, factors, old_limit, new_limit, picked, turn, key_rows, value_rows),
         (attention_gain, feedforward_gain),
         seq_count,
         blk_count,
     )
-    return (hidden_out, passage_keys[None], passage_values[None])
 
 
 def solution(mesh):

time: 147 us -> 144 us (0.980)
  Pallas kernels: 145 us -> 138 us
  local copies, waits for them, and re-layouts: 1.57 us -> 4.89 us
    pallas_call x1 -> x0, Pallas kernels: 12.3 us -> none  [attend(): pl.pallas_call(attention_kernel, grid=(head_count, total_rows // block),...]
    pallas_call x1, Pallas kernels: 94 us -> 99.9 us  [finish(): pl.pallas_call(functools.partial(finish_kernel, seq_count, blk_count), ou...]
    unnamed x1 -> x5, local copies, waits for them, and re-layouts: 1.57 us -> 4.89 us
where the time goes in v5:
time: 144 us
  Pallas kernels  138 us (96%)
  local copies, waits for them, and re-layouts  4.89 us (3%)
    pallas_call x1, Pallas kernels, finish(): pl.pallas_call(functools.partial(finish_kernel, seq_count, blk_count), ou...  99.9 us
    pallas_call x1, Pallas kernels, project(): pl.pallas_call(functools.partial(project_kernel, seq_count, blk_count), o...  38.6 us
    unnamed x5, local copies, waits for them, and re-layouts  4.89 us

profile of v5, /device:TPU:0, one launch (start us, length us, event | category | flops | bytes accessed | tf_op | source)
XLA Modules:
  0.0 144.0 jit_solution(17584372058525686477)
XLA Ops:
  0.6 38.6 %shard_map.202 = (bf16[4,128,1024]{2,1,0:T(8,128)(2,1)}, bf16[4,128,512]{2,1,0:T(8,128)(2,1)}, f32[4,128,1]{2,1,0:T(8,128)}, bf16[128,512]{1,0:T(8,128)(2,1)}, b...) custom-call(bf16[128,4096]{1,0:T(8,128)(2,1)} %states_ref.1, ...), custom_call_target="tpu_custom_call" | custom-call | tf_op jit(solution)/shard_map/pallas_call | solution.py:394
  39.2 99.9 %shard_map.203 = (bf16[16,4096]{1,0:T(8,128)(2,1)}, bf16[1,1024,512]{2,1,0:T(8,128)(2,1)}, bf16[1,1024,512]{2,1,0:T(8,128)(2,1)}) custom-call(bf16[512,1024]{1,0:T(8,128)(2,1)} %weight_ref.1, bf16[1376,1024]{1,0:T(8,128)(2,1)} %bitcast.7, bf16[1376,1024]{1,0:T(8,128)(2,1)} %bitcast.8, bf16[1376,1024]{1,0:T(8,128)(2,1)} %down_ref.1, ...), custom_call_target="tpu_custom_call" | custom-call | tf_op jit(solution)/shard_map/pallas_call | solution.py:780
  139.1 0.0 copy-start
  139.1 1.7 %copy.25 = bf16[16,4096]{1,0:T(8,128)(2,1)} copy(bf16[16,4096]{1,0:T(8,128)(2,1)} %get-tuple-element.24) | data formatting | bytes 262144
  140.8 2.3 %copy.26 = bf16[1,1024,512]{2,1,0:T(8,128)(2,1)} copy(bf16[1,1024,512]{2,1,0:T(8,128)(2,1)} %get-tuple-element.25) | data formatting | bytes 2097152
  143.0 0.0 copy-done
  143.0 1.0 copy.27
Async XLA Ops:
  139.1 3.9 %copy-start = (bf16[1,1024,512]{2,1,0:T(8,128)(2,1)S(1)}, bf16[1,1024,512]{2,1,0:T(8,128)(2,1)}, u32[]{:S(2)}) copy-start(bf16[1,1024,512]{2,1,0:T(8,128)(2,1)} %get-tuple-element.26) | copy-start | bytes 3145732
